TPU v7x, 512 devices: a whole 4x8x8 slice. The times are simulated.
512 devices in a mesh: sess: 16 (over y, core), band: 32 (over x, z).
Axes of the slice: x: 4, y: 8, z: 8, core: 2. Of those that a mesh axis runs over, the one named last changes fastest.
Arguments:
- frame: bfloat16 [64, 96, 128, 128], P('sess', None, 'band'), may hold values from -40 to 40
- cache: bfloat16 [64, 2, 2, 96, 128, 128], P('sess', None, None, None, 'band'), may hold values from -6 to 6
- holder_map: int32 [64], replicated, may hold values from 0 to 63, as said below
- counts: int32 [64], replicated, may hold values from 0 to 2
- active: int32 [64], replicated, may hold values 0 or 1
- weight_one: bfloat16 [96, 2592], replicated, may hold values from -0.125 to 0.125
- weight_two: bfloat16 [96, 2592], replicated, may hold values from -0.125 to 0.125
- gain_one: float32 [96], replicated, may hold values from 0.25 to 1.75
- gain_two: float32 [96], replicated, may hold values from 0.25 to 1.75
Outputs:
- block_out: bfloat16 [64, 96, 128, 128], P('sess', None, 'band')
Inputs may be any that keep to these rules, and one draw needn't show every extreme that they name: holder_map is a permutation of 0 to 63; slot k lies at sess index k // 4; the cache slots of the 4 sessions of one sess index lie at 4 different sess indices: at most one of them at any one sess index.
All inputs are finite; a program needn't handle non-finite values.
Results may differ from a plain program's by a relative error of at most 0.0016.
Values may be sent and summed in bfloat16 or wider, within the bound.
No kernel may reach another device: no remote copies, remote signals or barrier semaphores. Data moves between devices by JAX's collectives and lax.ppermute only.
A program may use at most 64 MiB of HBM per device.

v0:
```python
import jax
import jax.numpy as jnp
from jax import lax
from jax.sharding import PartitionSpec as P


def extended(cells, sides, width):
    for axis, dim in sides:
        count = lax.axis_size(axis)
        ends = count - 1
        head = lax.slice_in_dim(cells, 0, width, axis=dim)
        tail = lax.slice_in_dim(cells, cells.shape[dim] - width, cells.shape[dim], axis=dim)
        cells = jnp.concatenate(
            [
                lax.ppermute(tail, axis, [(i, (i + 1) % count) for i in range(ends)]),
                cells,
                lax.ppermute(head, axis, [((i + 1) % count, i) for i in range(ends)]),
            ],
            axis=dim,
        )
    return cells


def norm_silu(values, gain_vec):
    mean_square = jnp.mean(values * values, axis=1, keepdims=True)
    scaled = values * lax.rsqrt(mean_square + 1e-06) * gain_vec[None, :, None, None]
    return jax.nn.silu(scaled)


def causal_conv(frames_stack, weight):
    sessions, frame_count, channels, rows_in, width_cells = frames_stack.shape
    rows_out = rows_in - 2
    padded = jnp.pad(frames_stack, ((0, 0), (0, 0), (0, 0), (0, 0), (1, 1)))
    accum_out = jnp.zeros((sessions, channels, rows_out, width_cells), jnp.float32)
    for row_tap in range(3):
        pieces = [
            padded[:, time_tap, :, row_tap : row_tap + rows_out, col_tap : col_tap + width_cells]
            for time_tap in range(3)
            for col_tap in range(3)
        ]
        columns = jnp.concatenate(pieces, axis=1)
        weight_block = weight[:, row_tap * 9 * channels : (row_tap + 1) * 9 * channels]
        accum_out = accum_out + jnp.einsum(
            "ok,skrw->sorw", weight_block, columns, preferred_element_type=jnp.float32
        )
    return accum_out


def layer_conv(past_frames, current_act, weight):
    frames_stack = jnp.concatenate([past_frames, current_act[:, None]], axis=1)
    widened = extended(frames_stack, (("band", 3),), 1)
    return causal_conv(widened, weight)


def apply_live(slabs, slab_counts):
    live = jnp.arange(2, dtype=jnp.int32)[None, :] >= 2 - slab_counts[:, None]
    return jnp.where(live[:, None, :, None, None, None], slabs, jnp.zeros_like(slabs))


def pack_slots(payload, match):
    local_ids = jnp.arange(match.shape[1], dtype=jnp.int32)
    source = jnp.sum(jnp.where(match, local_ids[None, :], 0), axis=1)
    filled = jnp.any(match, axis=1)
    picked = jnp.take(payload, source, axis=0)
    tail_ones = (1,) * (payload.ndim - 1)
    return jnp.where(filled.reshape((-1,) + tail_ones), picked, jnp.zeros_like(picked))


def run_block(current, kept, weight_one, weight_two, gain_one, gain_two):
    act_one = norm_silu(current.astype(jnp.float32), gain_one).astype(jnp.bfloat16)
    hidden_one = layer_conv(kept[:, 0], act_one, weight_one)
    act_two = norm_silu(hidden_one, gain_two).astype(jnp.bfloat16)
    hidden_two = layer_conv(kept[:, 1], act_two, weight_two)
    return current.astype(jnp.float32) + hidden_two


def local(frame, cache, holder_map, counts, active, weight_one, weight_two, gain_one, gain_two):
    sess_count = lax.axis_size("sess")
    sess_index = lax.axis_index("sess")
    per_device = frame.shape[0]
    all_sessions = holder_map.shape[0]
    capacity = max(1, per_device // sess_count)
    session_ids = jnp.arange(all_sessions, dtype=jnp.int32)
    hits = holder_map[:, None] == session_ids[None, :]
    owner_of_slot = jnp.sum(jnp.where(hits, (session_ids // per_device)[:, None], 0), axis=0)
    owner_grid = owner_of_slot.reshape(sess_count, per_device)
    local_ids = jnp.arange(per_device, dtype=jnp.int32)
    earlier = local_ids[None, :, None] > local_ids[None, None, :]
    same_owner = owner_grid[:, :, None] == owner_grid[:, None, :]
    rank_of_slot = jnp.sum(same_owner & earlier, axis=2).reshape(all_sessions)
    send_position = owner_of_slot * capacity + rank_of_slot
    hold_position = session_ids // per_device * capacity + rank_of_slot
    start_row = sess_index * per_device
    local_send = lax.dynamic_slice_in_dim(send_position, start_row, per_device)
    my_slots = lax.dynamic_slice_in_dim(holder_map, start_row, per_device)
    receive_at = jnp.sum(
        jnp.where(session_ids[None, :] == my_slots[:, None], hold_position[None, :], 0), axis=1
    )
    positions = jnp.arange(sess_count * capacity, dtype=jnp.int32)
    send_match = positions[:, None] == local_send[None, :]
    my_active = lax.dynamic_slice_in_dim(active, start_row, per_device).astype(jnp.float32)
    outgoing = pack_slots(cache, send_match)
    arrived = lax.all_to_all(outgoing, "sess", split_axis=0, concat_axis=0, tiled=True)
    mine_cache = jnp.take(arrived, receive_at, axis=0)
    my_counts = lax.dynamic_slice_in_dim(counts, start_row, per_device)
    kept = apply_live(mine_cache, my_counts)
    result = run_block(frame, kept, weight_one, weight_two, gain_one, gain_two)
    return (my_active[:, None, None, None] * result).astype(jnp.bfloat16)


def solution(mesh):
    return jax.shard_map(
        local,
        mesh=mesh,
        in_specs=(
            P("sess", None, "band", None),
            P("sess", None, None, None, "band", None),
            P(),
            P(),
            P(),
            P(),
            P(),
            P(),
            P(),
        ),
        out_specs=P("sess", None, "band", None),
        check_vma=False,
    )
```

profile of v0, /device:TPU:7, one launch (start us, length us, event | category | flops | bytes accessed | tf_op | source)
XLA Modules:
  0.0 225.3 jit_solution(4196964103649030812)
XLA Ops:
  0.0 0.9 select_reduce_fusion
  1.6 7.4 %gather_fusion = bf16[16,2,2,96,4,128]{5,4,3,2,1,0:T(4,128)(2,1)} fusion(bf16[4,2,2,96,4,128]{5,4,3,2,1,0:T(4,128)(2,1)S(1)} %copy-done, s32[1024]{0:T(1024)S(1)} %pad_clamp_fusion.1), kind=kCustom, calls=%fused_computation | custom fusion | bytes 12582976 | tf_op jit(solution)/shard_map/jit(_take)/gather | solution.py:64
  9.0 8.5 %select_select_fusion = bf16[16,2,2,96,4,128]{5,4,3,2,1,0:T(4,128)(2,1)} fusion(bf16[16,2,2,96,4,128]{5,4,3,2,1,0:T(4,128)(2,1)} %gather_fusion, pred[16]{0:T(512)(128)(4,1)S(1)} %compare_and_fusion, pred[16]{0:T(512)(128)(4,1)S(1)} %fusion.98), kind=kLoop, calls=%fused_computation.5 | loop fusion | flops 6291456 | bytes 12582944 | tf_op jit(solution)/shard_map/jit(_where)/select_n | solution.py:66
  17.5 7.9 %all-to-all-start = ((bf16[16,2,2,96,4,128]{5,4,3,2,1,0:T(4,128)(2,1)}), bf16[16,2,2,96,4,128]{5,4,3,2,1,0:T(4,128)(2,1)}, u32[]{:S(2)}, u32[]{:S(2)}) async-start(bf16[16,2,2,96,4,128]{5,4,3,2,1,0:T(4,128)(2,1)} %select_select_fusion), calls=%async_computation | async-start | bytes 12582912 | tf_op jit(solution)/shard_map/all_to_all | solution.py:103
  25.6 0.2 select_reduce_fusion.2
  26.0 0.3 fusion.102
  26.3 137.7 %all-to-all-done = bf16[16,2,2,96,4,128]{5,4,3,2,1,0:T(4,128)(2,1)} async-done(((bf16[16,2,2,96,4,128]{5,4,3,2,1,0:T(4,128)(2,1)}), bf16[16,2,2,96,4,128]{5,4,3,2,1,0:T(4,128)(2,1)}, u32[]{:S(2)}, u32[]{:S(2)}) %all-to-all-start) | async-done | bytes 6291488 | tf_op jit(solution)/shard_map/all_to_all | solution.py:103
  164.0 7.1 %copy.23 = bf16[16,2,2,96,4,128]{5,3,4,2,1,0:T(8,128)(2,1)} copy(bf16[16,2,2,96,4,128]{5,4,3,2,1,0:T(4,128)(2,1)} %all-to-all-done) | data formatting | bytes 12582912 | tf_op jit(solution)/shard_map/all_to_all | solution.py:103
  171.1 3.6 %gather_fusion.1 = bf16[4,2,2,96,4,128]{5,3,4,2,1,0:T(8,128)(2,1)S(1)} fusion(bf16[16,2,2,96,4,128]{5,3,4,2,1,0:T(8,128)(2,1)} %copy.23, s32[1024]{0:T(1024)S(1)} %pad_clamp_fusion), kind=kCustom, calls=%fused_computation.1 | custom fusion | bytes 3145744 | tf_op jit(solution)/shard_map/jit(_take)/gather | solution.py:104
  174.7 0.2 fusion.11
  175.0 0.1 slice_bitcast_fusion.1
  175.2 4.0 %collective-permute-start = (bf16[4,3,96,1,128]{4,2,3,0,1:T(8,128)(2,1)S(1)}, bf16[4,3,96,1,128]{4,2,3,0,1:T(8,128)(2,1)S(1)}, u32[]{:S(2)}, u32[]{:S(2)}) collective-permute-start(bf16[4,3,96,1,128]{4,2,3,0,1:T(8,128)(2,1)S(1)} %get-tuple-element.57), channel_id=1, source_target_pairs={{0,1},{1,2},{2,3},{3,4},{4,5},{5,6},{6,7},{7,8},{8,9},{9,10},{10,1... | collective-permute-start | bytes 884744 | tf_op jit(solution)/shard_map/ppermute | solution.py:15
  179.2 9.0 %collective-permute-start.1 = (bf16[4,3,96,1,128]{4,2,3,0,1:T(8,128)(2,1)S(1)}, bf16[4,3,96,1,128]{4,2,3,0,1:T(8,128)(2,1)S(1)}, u32[]{:S(2)}, u32[]{:S(2)}) collective-permute-start(bf16[4,3,96,1,128]{4,2,3,0,1:T(8,128)(2,1)S(1)} %get-tuple-element.58), channel_id=1, source_target_pairs={{1,0},{2,1},{3,2},{4,3},{5,4},{6,5},{7,6},{8,7},{9,8},{10,9},{11,1... | collective-permute-start | bytes 884744 | tf_op jit(solution)/shard_map/ppermute | solution.py:17
  188.2 4.4 %collective-permute-done = bf16[4,3,96,1,128]{4,2,3,0,1:T(8,128)(2,1)S(1)} collective-permute-done((bf16[4,3,96,1,128]{4,2,3,0,1:T(8,128)(2,1)S(1)}, bf16[4,3,96,1,128]{4,2,3,0,1:T(8,128)(2,1)S(1)}, u32[]{:S(2)}, u32[]{:S(2)}) %collective-permute-start) | collective-permute-done | bytes 294944 | tf_op jit(solution)/shard_map/ppermute | solution.py:15
  192.6 0.9 collective-permute-done.1
  193.5 2.9 %fusion.8 = bf16[4,3,96,6,130]{4,2,3,0,1:T(8,128)(2,1)S(1)} fusion(bf16[4,3,96,1,128]{4,2,3,0,1:T(8,128)(2,1)S(1)} %collective-permute-done.1, bf16[4,3,96,1,128]{4,2,3,0,1:T(8,128)(2,1)S(1)} %collective-permute-done, bf16[4,1,96,4,128]{4,2,3,0,1:T(8,128)(2,1)S(1)} %fusion.102, bf16[4,2,96,4,128]{4,2,3,0,1:T(8,128)(2,1)S(1)} %get-tuple-element.42), kind=kLoop, calls=%fused_computation.15 | loop fusion | flops 13478400 | bytes 3566592 | tf_op jit(solution)/shard_map/concatenate | solution.py:13
  196.4 0.2 fusion.65
  196.6 0.3 fusion.64
  196.8 0.6 fusion.63
  197.4 0.3 fusion.62
  197.7 0.3 fusion.61
  198.0 0.6 fusion.60
  198.6 0.3 fusion.59
  198.9 0.4 fusion.58
  199.3 0.6 fusion.56
  199.9 0.8 fusion.89
  200.7 0.8 convolution_add_fusion.3
  201.5 0.8 multiply_reduce_fusion
  202.3 0.3 fusion.109
  202.7 1.9 collective-permute-start.2
  204.7 6.4 %collective-permute-start.3 = (bf16[4,3,96,1,128]{4,2,3,0,1:T(8,128)(2,1)S(1)}, bf16[4,3,96,1,128]{4,2,3,0,1:T(8,128)(2,1)S(1)}, u32[]{:S(2)}, u32[]{:S(2)}) collective-permute-start(bf16[4,3,96,1,128]{4,2,3,0,1:T(8,128)(2,1)S(1)} %get-tuple-element.50), channel_id=1, source_target_pairs={{1,0},{2,1},{3,2},{4,3},{5,4},{6,5},{7,6},{8,7},{9,8},{10,9},{11,1... | collective-permute-start | bytes 884744 | tf_op jit(solution)/shard_map/ppermute | solution.py:17
  211.2 3.3 %collective-permute-done.2 = bf16[4,3,96,1,128]{4,2,3,0,1:T(8,128)(2,1)S(1)} collective-permute-done((bf16[4,3,96,1,128]{4,2,3,0,1:T(8,128)(2,1)S(1)}, bf16[4,3,96,1,128]{4,2,3,0,1:T(8,128)(2,1)S(1)}, u32[]{:S(2)}, u32[]{:S(2)}) %collective-permute-start.2) | collective-permute-done | bytes 294944 | tf_op jit(solution)/shard_map/ppermute | solution.py:15
  214.5 0.9 collective-permute-done.3
  215.4 2.9 %select_maximum_fusion = bf16[4,3,96,6,130]{4,2,3,0,1:T(8,128)(2,1)S(1)} fusion(bf16[4,3,96,1,128]{4,2,3,0,1:T(8,128)(2,1)S(1)} %collective-permute-done.3, bf16[4,3,96,1,128]{4,2,3,0,1:T(8,128)(2,1)S(1)} %collective-permute-done.2, bf16[4,1,96,4,128]{4,2,3,0,1:T(8,128)(2,1)S(1)} %fusion.109, bf16[4,2,96,4,128]{4,2,3,0,1:T(8,128)(2,1)S(1)} %get-tuple-element.41), kind=kLoop, calls=%fused_computation.6 | loop fusion | flops 13478400 | bytes 3566592 | tf_op jit(solution)/shard_map/concatenate | solution.py:13
  218.3 0.2 fusion.37
  218.5 0.3 fusion.36
  218.7 0.6 fusion.35
  219.4 0.3 fusion.34
  219.6 0.3 fusion.33
  219.9 0.6 fusion.32
  220.5 0.3 fusion.31
  220.8 0.3 constant_dynamic-update-slice_fusion.1
  221.1 0.2 fusion.30
  221.3 0.6 fusion.28
  221.9 0.8 fusion.85
  222.7 0.8 convolution_add_fusion.1
  223.5 0.8 fusion.15
  224.3 0.9 copy.25
  (46 shorter events, 1.3 us)
Async XLA Ops:
  0.0 1.6 copy-start
  17.5 7.9 %copy-start.7 = (s32[64]{0:T(128)S(1)}, s32[64]{0:T(128)}, u32[]{:S(2)}) copy-start(s32[64]{0:T(128)} %param.11) | copy-start | bytes 772
  17.5 8.0 %copy-start.8 = (s32[64]{0:T(128)S(1)}, s32[64]{0:T(128)}, u32[]{:S(2)}) copy-start(s32[64]{0:T(128)} %param.12) | copy-start | bytes 772
  17.5 8.3 %copy-start.2 = (bf16[4,96,4,128]{3,2,1,0:T(4,128)(2,1)S(1)}, bf16[4,96,4,128]{3,2,1,0:T(4,128)(2,1)}, u32[]{:S(2)}) copy-start(bf16[4,96,4,128]{3,2,1,0:T(4,128)(2,1)} %param.9) | copy-start | bytes 1179652
  17.5 8.5 %copy-start.6 = (f32[96]{0:T(128)S(1)}, f32[96]{0:T(128)}, u32[]{:S(2)}) copy-start(f32[96]{0:T(128)} %param.16) | copy-start | bytes 1156
  17.5 146.5 %all-to-all-start = ((bf16[16,2,2,96,4,128]{5,4,3,2,1,0:T(4,128)(2,1)}), bf16[16,2,2,96,4,128]{5,4,3,2,1,0:T(4,128)(2,1)}, u32[]{:S(2)}, u32[]{:S(2)}) async-start(bf16[16,2,2,96,4,128]{5,4,3,2,1,0:T(4,128)(2,1)} %select_select_fusion), calls=%async_computation | async-start | bytes 12582912 | tf_op jit(solution)/shard_map/all_to_all | solution.py:103
  175.2 17.4 %collective-permute-start = (bf16[4,3,96,1,128]{4,2,3,0,1:T(8,128)(2,1)S(1)}, bf16[4,3,96,1,128]{4,2,3,0,1:T(8,128)(2,1)S(1)}, u32[]{:S(2)}, u32[]{:S(2)}) collective-permute-start(bf16[4,3,96,1,128]{4,2,3,0,1:T(8,128)(2,1)S(1)} %get-tuple-element.57), channel_id=1, source_target_pairs={{0,1},{1,2},{2,3},{3,4},{4,5},{5,6},{6,7},{7,8},{8,9},{9,10},{10,1... | collective-permute-start | bytes 884744 | tf_op jit(solution)/shard_map/ppermute | solution.py:15
  179.2 14.3 %collective-permute-start.1 = (bf16[4,3,96,1,128]{4,2,3,0,1:T(8,128)(2,1)S(1)}, bf16[4,3,96,1,128]{4,2,3,0,1:T(8,128)(2,1)S(1)}, u32[]{:S(2)}, u32[]{:S(2)}) collective-permute-start(bf16[4,3,96,1,128]{4,2,3,0,1:T(8,128)(2,1)S(1)} %get-tuple-element.58), channel_id=1, source_target_pairs={{1,0},{2,1},{3,2},{4,3},{5,4},{6,5},{7,6},{8,7},{9,8},{10,9},{11,1... | collective-permute-start | bytes 884744 | tf_op jit(solution)/shard_map/ppermute | solution.py:17
  198.6 1.3 copy-start.3
  201.5 0.9 copy-start.5
  201.5 9.6 %copy-start.9 = (s32[64]{0:T(128)S(1)}, s32[64]{0:T(128)}, u32[]{:S(2)}) copy-start(s32[64]{0:T(128)} %param.13) | copy-start | bytes 772
  202.7 11.8 %collective-permute-start.2 = (bf16[4,3,96,1,128]{4,2,3,0,1:T(8,128)(2,1)S(1)}, bf16[4,3,96,1,128]{4,2,3,0,1:T(8,128)(2,1)S(1)}, u32[]{:S(2)}, u32[]{:S(2)}) collective-permute-start(bf16[4,3,96,1,128]{4,2,3,0,1:T(8,128)(2,1)S(1)} %get-tuple-element.49), channel_id=1, source_target_pairs={{0,1},{1,2},{2,3},{3,4},{4,5},{5,6},{6,7},{7,8},{8,9},{9,10},{10,1... | collective-permute-start | bytes 884744 | tf_op jit(solution)/shard_map/ppermute | solution.py:15
  204.7 10.7 %collective-permute-start.3 = (bf16[4,3,96,1,128]{4,2,3,0,1:T(8,128)(2,1)S(1)}, bf16[4,3,96,1,128]{4,2,3,0,1:T(8,128)(2,1)S(1)}, u32[]{:S(2)}, u32[]{:S(2)}) collective-permute-start(bf16[4,3,96,1,128]{4,2,3,0,1:T(8,128)(2,1)S(1)} %get-tuple-element.50), channel_id=1, source_target_pairs={{1,0},{2,1},{3,2},{4,3},{5,4},{6,5},{7,6},{8,7},{9,8},{10,9},{11,1... | collective-permute-start | bytes 884744 | tf_op jit(solution)/shard_map/ppermute | solution.py:17
  220.8 1.1 copy-start.4
  222.7 2.5 %copy-start.1 = (bf16[4,2,2,96,4,128]{5,4,3,2,1,0:T(4,128)(2,1)S(1)}, bf16[4,2,2,96,4,128]{5,4,3,2,1,0:T(4,128)(2,1)}, u32[]{:S(2)}) copy-start(bf16[4,2,2,96,4,128]{5,4,3,2,1,0:T(4,128)(2,1)} %param.10) | copy-start | bytes 4718596
where the time goes:
time: 228 us; the launch traced here: 225 us
  waiting for transfers between devices  147 us (64%)
  starting transfers between devices  29.3 us (13%)
  local copies, waits for them, and re-layouts  24.9 us (11%)
  other arithmetic  18.7 us (8%)
  matrix products  4.72 us (2%)
    all_to_all x1, waiting for transfers between devices, local(): lax.all_to_all(outgoing, 'sess', split_axis=0, concat_axis=0, tiled=True)  138 us
    ppermute x2, starting transfers between devices, extended(): lax.ppermute(head, axis, [((i + 1) % count, i) for i in range(ends)])  15.5 us
    select_n x1, other arithmetic, pack_slots(): jnp.where(filled.reshape((-1,) + tail_ones), picked, jnp.zeros_like(picked))  8.48 us
    all_to_all x1, starting transfers between devices, local(): lax.all_to_all(outgoing, 'sess', split_axis=0, concat_axis=0, tiled=True)  7.93 us
    ppermute x2, waiting for transfers between devices, extended(): lax.ppermute(tail, axis, [(i, (i + 1) % count) for i in range(ends)])  7.68 us
    gather x1, local copies, waits for them, and re-layouts, pack_slots(): picked = jnp.take(payload, source, axis=0)  7.36 us
    all_to_all x1, local copies, waits for them, and re-layouts, local(): lax.all_to_all(outgoing, 'sess', split_axis=0, concat_axis=0, tiled=True)  7.14 us
    ppermute x2, starting transfers between devices, extended(): lax.ppermute(tail, axis, [(i, (i + 1) % count) for i in range(ends)])  5.92 us
  transfers between devices with their start and end apart: 5, of which 5 were waited for; matrix products, arithmetic and copies ran while one was open for 0% of the time, Pallas kernels for 0%

commit v1 on v0

v1 whole, which is shorter than its diff:
```python
import jax
import jax.numpy as jnp
from jax import lax
from jax.experimental import pallas as pl
from jax.experimental.pallas import tpu as pltpu
from jax.sharding import PartitionSpec as P

F32 = jnp.float32
BF16 = jnp.bfloat16


def three_taps(values):
    width = values.shape[1]
    column = lax.broadcasted_iota(jnp.int32, values.shape, 1)
    before = jnp.where(column == 0, 0.0, pltpu.roll(values, 1, 1))
    after = jnp.where(column == width - 1, 0.0, pltpu.roll(values, width - 1, 1))
    return before.astype(BF16), values.astype(BF16), after.astype(BF16)


def store_taps(cols_ref, at, channels, half, values):
    width = values.shape[1]
    for tap, moved in enumerate(three_taps(values)):
        cols_ref[at + tap * channels : at + (tap + 1) * channels, half * width : (half + 1) * width] = moved


def norm_silu(values, gain):
    mean_square = jnp.mean(values * values, axis=0, keepdims=True)
    scaled = values * lax.rsqrt(mean_square + 1e-06) * gain
    return scaled / (1.0 + jnp.exp(-scaled))


def past_kernel(live_ref, own_ref, above_ref, below_ref, w_one_ref, w_two_ref, one_ref, two_ref, cols_ref):
    pair = pl.program_id(0)
    rows, channels = own_ref.shape[3], own_ref.shape[4]
    step = 2 * 3 * channels

    def fill(slot, half, frame, source):
        keep = live_ref[2 * (2 * pair + half) + frame]
        values = source.astype(F32) * keep.astype(F32)
        store_taps(cols_ref, slot * step + frame * 3 * channels, channels, half, values)

    for half in range(2):
        for frame in range(2):
            for slot in range(rows + 4):
                if slot < 2:
                    source = above_ref[half, frame, slot]
                elif slot < rows + 2:
                    source = own_ref[0, half, frame, slot - 2]
                else:
                    source = below_ref[half, frame, slot - rows - 2]
                fill(slot, half, frame, source)
    for row in range(rows + 2):
        one_ref[0, row] = jnp.dot(w_one_ref[...], cols_ref[row * step : (row + 3) * step, :], preferred_element_type=F32)
    for half in range(2):
        for frame in range(2):
            for slot in range(rows + 2):
                if slot < 1:
                    source = above_ref[half, frame, 2]
                elif slot < rows + 1:
                    source = own_ref[1, half, frame, slot - 1]
                else:
                    source = below_ref[half, frame, 2]
                fill(slot, half, frame, source)
    for row in range(rows):
        two_ref[0, row] = jnp.dot(w_two_ref[...], cols_ref[row * step : (row + 3) * step, :], preferred_element_type=F32)


def past_sums(live, own, above, below, w_one, w_two):
    _, sessions, frames, rows, channels, width = own.shape
    pairs = sessions // 2
    whole = lambda p, live: (0, 0)
    return pl.pallas_call(
        past_kernel,
        grid_spec=pltpu.PrefetchScalarGridSpec(
            num_scalar_prefetch=1,
            grid=(pairs,),
            in_specs=[
                pl.BlockSpec((2, 2, frames, rows, channels, width), lambda p, live: (0, p, 0, 0, 0, 0)),
                pl.BlockSpec((2, frames, 3, channels, width), lambda p, live: (p, 0, 0, 0, 0)),
                pl.BlockSpec((2, frames, 3, channels, width), lambda p, live: (p, 0, 0, 0, 0)),
                pl.BlockSpec(w_one.shape, whole),
                pl.BlockSpec(w_two.shape, whole),
            ],
            out_specs=[
                pl.BlockSpec((1, rows + 2, channels, 2 * width), lambda p, live: (p, 0, 0, 0)),
                pl.BlockSpec((1, rows, channels, 2 * width), lambda p, live: (p, 0, 0, 0)),
            ],
            scratch_shapes=[pltpu.VMEM(((rows + 4) * 6 * channels, 2 * width), BF16)],
        ),
        out_shape=[
            jax.ShapeDtypeStruct((pairs, rows + 2, channels, 2 * width), F32),
            jax.ShapeDtypeStruct((pairs, rows, channels, 2 * width), F32),
        ],
        compiler_params=pltpu.CompilerParams(vmem_limit_bytes=40 * 1024 * 1024),
        cost_estimate=pl.CostEstimate(flops=4 * 10**9, bytes_accessed=6 * 10**6, transcendentals=0),
        name="past_sums",
    )(live, own, above, below, w_one, w_two)


def act_kernel(flags_ref, own_ref, above_ref, below_ref, one_ref, two_ref, w_one_ref, w_two_ref, g_one_ref, g_two_ref, out_ref, cols_ref):
    pair = pl.program_id(0)
    channels, width = w_one_ref.shape[0], own_ref.shape[3]
    part = own_ref.shape[2]
    parts = channels // part
    rows = own_ref.shape[0] // parts
    step = 3 * channels

    def frame_row(ref, row, half):
        return jnp.concatenate([ref[row * parts + q, half].astype(F32) for q in range(parts)], axis=0)

    g_one, g_two = g_one_ref[...], g_two_ref[...]
    for half in range(2):
        for slot in range(rows + 4):
            if slot < 2:
                values = frame_row(above_ref, slot, half)
            elif slot < rows + 2:
                values = frame_row(own_ref, slot - 2, half)
            else:
                values = frame_row(below_ref, slot - rows - 2, half)
            store_taps(cols_ref, slot * step, channels, half, norm_silu(values, g_one))
    acts = []
    for row in range(rows + 2):
        hidden = one_ref[0, row] + jnp.dot(
            w_one_ref[...], cols_ref[row * step : (row + 3) * step, :], preferred_element_type=F32
        )
        act = norm_silu(hidden, g_two)
        if row == 0:
            act = act * flags_ref[0].astype(F32)
        elif row == rows + 1:
            act = act * flags_ref[1].astype(F32)
        base = (rows + 4) * step + row * step
        for half in range(2):
            store_taps(cols_ref, base, channels, half, act[:, half * width : (half + 1) * width])
    for row in range(rows):
        base = (rows + 4) * step + row * step
        hidden = two_ref[0, row] + jnp.dot(
            w_two_ref[...], cols_ref[base : base + 3 * step, :], preferred_element_type=F32
        )
        for half in range(2):
            active = flags_ref[2 + 2 * pair + half].astype(F32)
            total = active * (frame_row(own_ref, row, half) + hidden[:, half * width : (half + 1) * width])
            for q in range(parts):
                out_ref[row * parts + q, half] = total[q * part : (q + 1) * part].astype(BF16)


def act_block(flags, own, above, below, one, two, w_one, w_two, g_one, g_two):
    pieces, sessions, part, width = own.shape
    pairs, rows, channels, _ = two.shape
    whole = lambda p, flags: (0, 0)
    piece_block = lambda count: pl.BlockSpec((count, 2, part, width), lambda p, flags: (0, p, 0, 0))
    return pl.pallas_call(
        act_kernel,
        grid_spec=pltpu.PrefetchScalarGridSpec(
            num_scalar_prefetch=1,
            grid=(pairs,),
            in_specs=[
                piece_block(pieces),
                piece_block(above.shape[0]),
                piece_block(below.shape[0]),
                pl.BlockSpec((1,) + one.shape[1:], lambda p, flags: (p, 0, 0, 0)),
                pl.BlockSpec((1,) + two.shape[1:], lambda p, flags: (p, 0, 0, 0)),
                pl.BlockSpec(w_one.shape, whole),
                pl.BlockSpec(w_two.shape, whole),
                pl.BlockSpec(g_one.shape, whole),
                pl.BlockSpec(g_two.shape, whole),
            ],
            out_specs=piece_block(pieces),
            scratch_shapes=[pltpu.VMEM(((2 * rows + 6) * 3 * channels, 2 * width), BF16)],
        ),
        out_shape=jax.ShapeDtypeStruct(own.shape, BF16),
        compiler_params=pltpu.CompilerParams(vmem_limit_bytes=40 * 1024 * 1024),
        cost_estimate=pl.CostEstimate(flops=2 * 10**9, bytes_accessed=4 * 10**6, transcendentals=10**6),
        name="act_block",
    )(flags, own, above, below, one, two, w_one, w_two, g_one, g_two)


def scatter_kernel(map_ref, in_ref, out_ref):
    def body(i, carry):
        out_ref[map_ref[i]] = in_ref[i]
        return carry

    lax.fori_loop(0, in_ref.shape[0], body, 0, unroll=8)


def gather_kernel(map_ref, in_ref, out_ref):
    def body(i, carry):
        out_ref[i] = in_ref[map_ref[i]]
        return carry

    lax.fori_loop(0, in_ref.shape[0], body, 0, unroll=8)


def reorder(kernel, slots, pieces, name):
    spec = pl.BlockSpec(pieces.shape, lambda i, slots: (0, 0, 0))
    return pl.pallas_call(
        kernel,
        grid_spec=pltpu.PrefetchScalarGridSpec(num_scalar_prefetch=1, grid=(1,), in_specs=[spec], out_specs=spec),
        out_shape=jax.ShapeDtypeStruct(pieces.shape, pieces.dtype),
        name=name,
    )(slots, pieces)


def exchange(pieces):
    return lax.all_to_all(pieces, "sess", 0, 0, tiled=True)


def local(frame, cache, holder_map, counts, active, weight_one, weight_two, gain_one, gain_two):
    sess_count, band_count = lax.axis_size("sess"), lax.axis_size("band")
    me, band = lax.axis_index("sess"), lax.axis_index("band")
    sessions, channels, rows, width = frame.shape
    parts = sess_count // rows
    part = channels // parts
    down = [(i, i + 1) for i in range(band_count - 1)]
    up = [(i + 1, i) for i in range(band_count - 1)]

    my_slots = me * sessions + jnp.arange(sessions, dtype=jnp.int32)
    here = holder_map[None, :] == my_slots[:, None]
    my_counts = jnp.sum(jnp.where(here, counts[None, :], 0), axis=1)
    my_active = jnp.sum(jnp.where(here, active[None, :], 0), axis=1)
    live = (jnp.arange(2, dtype=jnp.int32)[None, :] >= 2 - my_counts[:, None]).astype(jnp.int32).reshape(-1)
    flags = jnp.concatenate([jnp.stack([band > 0, band < band_count - 1]).astype(jnp.int32), my_active])

    cut = frame.reshape(sessions, parts, part, rows, width).transpose(3, 1, 0, 2, 4)
    spread = exchange(cut.reshape(sess_count, sessions, part, width))

    own = cache.transpose(1, 0, 2, 4, 3, 5)
    above = lax.ppermute(jnp.concatenate([own[0, :, :, rows - 2 :], own[1, :, :, rows - 1 :]], axis=2), "band", down)
    below = lax.ppermute(jnp.concatenate([own[0, :, :, :2], own[1, :, :, :1]], axis=2), "band", up)
    w_one = weight_one.reshape(channels, 3, 3, 3 * channels)
    w_two = weight_two.reshape(channels, 3, 3, 3 * channels)
    past_w = lambda w: w[:, :, :2].reshape(channels, -1)
    new_w = lambda w: w[:, :, 2].reshape(channels, -1)
    one, two = past_sums(live, own, above, below, past_w(w_one), past_w(w_two))

    sorted_pieces = reorder(scatter_kernel, holder_map, spread.reshape(-1, part, width), "to_holders")
    held = exchange(sorted_pieces.reshape(sess_count, sessions, part, width))
    half = sess_count - 2 * parts
    held_above = lax.ppermute(held[half:], "band", down)
    held_below = lax.ppermute(held[: 2 * parts], "band", up)
    result = act_block(
        flags, held, held_above, held_below, one, two, new_w(w_one), new_w(w_two), gain_one[:, None], gain_two[:, None]
    )

    spread_result = exchange(result)
    home_pieces = reorder(gather_kernel, holder_map, spread_result.reshape(-1, part, width), "to_homes")
    home = exchange(home_pieces.reshape(sess_count, sessions, part, width))
    home = home.reshape(rows, parts, sessions, part, width).transpose(2, 1, 3, 0, 4)
    return home.reshape(sessions, channels, rows, width)


def solution(mesh):
    return jax.shard_map(
        local,
        mesh=mesh,
        in_specs=(
            P("sess", None, "band", None),
            P("sess", None, None, None, "band", None),
            P(),
            P(),
            P(),
            P(),
            P(),
            P(),
            P(),
        ),
        out_specs=P("sess", None, "band", None),
        check_vma=False,
    )
```

time: 228 us -> 113 us (0.50)
  waiting for transfers between devices: 147 us -> 13.4 us
  blocking collectives: 0 us -> 35.5 us
  other arithmetic: 18.7 us -> 2.18 us
  Pallas kernels: 0 us -> 13.7 us
  local copies, waits for them, and re-layouts: 24.9 us -> 13.2 us
  matrix products: 4.72 us -> 0 us
  starting transfers between devices: 29.3 us -> 33.7 us
    all_to_all x1 -> x2, waiting for transfers between devices: 138 us -> 9.44 us  [exchange(): return lax.all_to_all(pieces, 'sess', 0, 0, tiled=True)]
    all_to_all x0 -> x2, blocking collectives: none -> 35.5 us  [exchange(): return lax.all_to_all(pieces, 'sess', 0, 0, tiled=True)]
    pallas_call x0 -> x4, Pallas kernels: none -> 13.7 us  [the longest x2 5.14 us: reorder(): pl.pallas_call(kernel, grid_spec=pltpu.PrefetchScalarGridSpec(num_scalar_...]
    gather x2 -> x0, local copies, waits for them, and re-layouts: 11 us -> none  [the longest x1 7.36 us: pack_slots(): picked = jnp.take(payload, source, axis=0)]
    select_n x5 -> x0, other arithmetic: 8.73 us -> none  [the longest x1 8.48 us: pack_slots(): jnp.where(filled.reshape((-1,) + tail_ones), picked, jnp.zeros_like(picked))]
    all_to_all x1 -> x2, starting transfers between devices: 7.93 us -> 15.3 us  [exchange(): return lax.all_to_all(pieces, 'sess', 0, 0, tiled=True)]
    all_to_all x1 -> x0, local copies, waits for them, and re-layouts: 7.14 us -> none  [local(): lax.all_to_all(outgoing, 'sess', split_axis=0, concat_axis=0, tiled=True)]
    ppermute x4, waiting for transfers between devices: 9.44 us -> 3.92 us  [the longest x1 3.92 us: local(): held_above = lax.ppermute(held[half:], 'band', down)]
  transfers between devices with their start and end apart: 5 -> 6, of which waited for: 5 -> 2; matrix products, arithmetic and copies ran while one was open for 0% -> 11% of each run, Pallas kernels for 0% -> 7%
where the time goes in v1:
time: 113 us; the launch traced here: 112 us
  blocking collectives  35.5 us (31%)
  starting transfers between devices  33.7 us (30%)
  Pallas kernels  13.7 us (12%)
  waiting for transfers between devices  13.4 us (12%)
  local copies, waits for them, and re-layouts  13.2 us (12%)
  other arithmetic  2.18 us (2%)
    all_to_all x2, blocking collectives, exchange(): return lax.all_to_all(pieces, 'sess', 0, 0, tiled=True)  35.5 us
    all_to_all x2, starting transfers between devices, exchange(): return lax.all_to_all(pieces, 'sess', 0, 0, tiled=True)  15.3 us
    all_to_all x2, waiting for transfers between devices, exchange(): return lax.all_to_all(pieces, 'sess', 0, 0, tiled=True)  9.44 us
    ppermute x1, starting transfers between devices, local(): lax.ppermute(jnp.concatenate([own[0, :, :, :2], own[1, :, :, :1]], axis=2...  8.84 us
    pallas_call x2, Pallas kernels, reorder(): pl.pallas_call(kernel, grid_spec=pltpu.PrefetchScalarGridSpec(num_scalar_...  5.14 us
    pallas_call x1, Pallas kernels, past_sums(): pl.pallas_call(past_kernel, grid_spec=pltpu.PrefetchScalarGridSpec(num_sc...  4.99 us
    ppermute x1, starting transfers between devices, local(): lax.ppermute(jnp.concatenate([own[0, :, :, rows - 2:], own[1, :, :, rows...  3.99 us
    ppermute x1, waiting for transfers between devices, local(): held_above = lax.ppermute(held[half:], 'band', down)  3.92 us
  transfers between devices with their start and end apart: 6, of which 2 were waited for; matrix products, arithmetic and copies ran while one was open for 11% of the time, Pallas kernels for 7%

profile of v1, /device:TPU:7, one launch (start us, length us, event | category | flops | bytes accessed | tf_op | source)
XLA Modules:
  0.0 111.8 jit_solution(7882865013949915586)
XLA Ops:
  0.0 1.9 %copy.34 = bf16[4,4,4,24,128]{4,3,2,1,0:T(8,128)(2,1)} copy(bf16[4,4,4,24,128]{4,0,3,1,2:T(4,128)(2,1)} %bitcast.51) | data formatting | bytes 786432 | tf_op jit(solution)/shard_map/transpose | solution.py:223
  1.9 7.8 %all-to-all-start = ((bf16[16,4,24,128]{3,2,1,0:T(8,128)(2,1)}), bf16[16,4,24,128]{3,2,1,0:T(8,128)(2,1)}, u32[]{:S(2)}, u32[]{:S(2)}) async-start(bf16[16,4,24,128]{3,2,1,0:T(8,128)(2,1)} %bitcast.4), calls=%async_computation | async-start | bytes 786432 | tf_op jit(solution)/shard_map/all_to_all | solution.py:204
  9.7 0.4 copy.56
  10.1 0.1 slice_bitcast_fusion
  10.2 0.0 copy-start.4
  10.2 0.9 pad_maximum_fusion
  11.1 4.0 %collective-permute-start.2 = (bf16[4,2,3,96,128]{4,3,1,0,2:T(8,128)(2,1)}, bf16[4,2,3,96,128]{4,3,1,0,2:T(8,128)(2,1)}, u32[]{:S(2)}, u32[]{:S(2)}) collective-permute-start(bf16[4,2,3,96,128]{4,3,1,0,2:T(8,128)(2,1)} %pad_maximum_fusion), channel_id=1, source_target_pairs={{0,1},{1,2},{2,3},{3,4},{4,5},{5,6},{6,7},{7,8},{8,9},{9,10},{10,1... | collective-permute-start | bytes 1769480 | tf_op jit(solution)/shard_map/ppermute | solution.py:227
  15.1 0.9 pad_maximum_fusion.1
  15.9 8.8 %collective-permute-start.3 = (bf16[4,2,3,96,128]{4,3,2,1,0:T(8,128)(2,1)}, bf16[4,2,3,96,128]{4,3,2,1,0:T(8,128)(2,1)}, u32[]{:S(2)}, u32[]{:S(2)}) collective-permute-start(bf16[4,2,3,96,128]{4,3,2,1,0:T(8,128)(2,1)} %pad_maximum_fusion.1), channel_id=1, source_target_pairs={{1,0},{2,1},{3,2},{4,3},{5,4},{6,5},{7,6},{8,7},{9,8},{10,9},{11,1... | collective-permute-start | bytes 1769480 | tf_op jit(solution)/shard_map/ppermute | solution.py:228
  24.8 0.3 copy.37
  25.1 0.7 slice.48
  25.8 0.8 slice.46
  26.6 1.4 %copy.39 = bf16[96,2592]{0,1:T(8,128)(2,1)S(1)} copy(bf16[96,2592]{1,0:T(8,128)(2,1)} %param.15) | data formatting | bytes 995328 | tf_op args[6]
  28.0 0.7 slice.49
  28.7 0.8 slice.47
  29.5 0.3 copy.55
  29.9 0.0 copy-start.5
  29.9 0.0 copy-start.8
  29.9 0.0 copy-start.9
  29.9 0.0 copy-start.6
  29.9 0.0 copy-start.7
  30.0 0.0 all-to-all-done
  30.0 2.6 %to_holders.1 = bf16[64,24,128]{2,1,0:T(8,128)(2,1)} custom-call(s32[64]{0:T(128)} %map_ref.3, bf16[64,24,128]{2,1,0:T(8,128)(2,1)} %bitcast.5.in_ref), custom_call_target="tpu_custom_call" | custom-call | tf_op jit(solution)/shard_map/to_holders/pallas_call | solution.py:195
  32.6 7.5 %all-to-all-start.1 = ((bf16[16,4,24,128]{3,2,1,0:T(8,128)(2,1)}), bf16[16,4,24,128]{3,2,1,0:T(8,128)(2,1)S(1)}, u32[]{:S(2)}, u32[]{:S(2)}) async-start(bf16[16,4,24,128]{3,2,1,0:T(8,128)(2,1)} %bitcast.46), calls=%async_computation.1 | async-start | bytes 786432 | tf_op jit(solution)/shard_map/all_to_all | solution.py:204
  40.1 0.2 fusion.1
  40.3 0.1 fusion.2
  40.4 0.1 reshape.65.live_ref
  40.5 0.1 copy.45.g_one_ref
  40.6 0.1 copy.46.g_two_ref
  40.7 0.2 copy.49.w_one_ref
  40.9 1.1 copy.43.w_one_ref
  42.0 0.2 copy.50.w_two_ref
  42.2 1.7 %copy.44.w_two_ref = bf16[96,864]{1,0:T(8,128)(2,1)} copy(bf16[96,864]{0,1:T(8,128)(2,1)} %bitcast.50) | data formatting | bytes 331776 | tf_op jit(solution)/shard_map/reshape;squeeze | solution.py:232
  44.0 0.1 add_convert_fusion
  44.0 0.1 pad_add_fusion.flags_ref
  44.1 0.0 collective-permute-done.2
  44.1 1.1 copy.42.above_ref
  45.2 9.4 %all-to-all-done.1.own_ref = bf16[16,4,24,128]{3,2,1,0:T(8,128)(2,1)S(1)} async-done(((bf16[16,4,24,128]{3,2,1,0:T(8,128)(2,1)}), bf16[16,4,24,128]{3,2,1,0:T(8,128)(2,1)S(1)}, u32[]{:S(2)}, u32[]{:S(2)}) %all-to-all-start.1) | async-done | bytes 393248 | tf_op jit(solution)/shard_map/all_to_all | solution.py:204
  54.7 3.6 %collective-permute-start.1 = (bf16[8,4,24,128]{3,2,1,0:T(8,128)(2,1)S(1)}, bf16[8,4,24,128]{3,2,1,0:T(8,128)(2,1)S(1)}, u32[]{:S(2)}, u32[]{:S(2)}) collective-permute-start(bf16[8,4,24,128]{3,2,1,0:T(8,128)(2,1)S(1)} %get-tuple-element.15), channel_id=1, source_target_pairs={{1,0},{2,1},{3,2},{4,3},{5,4},{6,5},{7,6},{8,7},{9,8},{10,9},{11,1... | collective-permute-start | bytes 589832 | tf_op jit(solution)/shard_map/ppermute | solution.py:239
  58.4 1.9 %collective-permute-start = (bf16[8,4,24,128]{3,2,1,0:T(8,128)(2,1)S(1)}, bf16[8,4,24,128]{3,2,1,0:T(8,128)(2,1)S(1)}, u32[]{:S(2)}, u32[]{:S(2)}) collective-permute-start(bf16[8,4,24,128]{3,2,1,0:T(8,128)(2,1)S(1)} %get-tuple-element.16), channel_id=1, source_target_pairs={{0,1},{1,2},{2,3},{3,4},{4,5},{5,6},{6,7},{7,8},{8,9},{9,10},{10,1... | collective-permute-start | bytes 589832 | tf_op jit(solution)/shard_map/ppermute | solution.py:238
  60.3 5.0 %past_sums.1 = (f32[2,6,96,256]{3,2,1,0:T(8,128)S(1)}, f32[2,4,96,256]{3,2,1,0:T(8,128)S(1)}) custom-call(s32[8]{0:T(128)S(1)} %reshape.65.live_ref, bf16[2,4,2,4,96,128]{5,4,3,2,1,0:T(8,128)(2,1)S(1)} %bitcast.36, bf16[4,2,3,96,128]{4,3,2,1,0:T(8,128)(2,1)S(1)} %copy.42.above_ref, bf16[4,2,3,96,128]{4,3,2,1,0:T(8,128)(2,1)} %collective-permute-done.3.below_ref, ...), custom_call_target="tpu_custom_call" | custom-call | flops 4000000000 | bytes 6000000 | tf_op jit(solution)/shard_map/past_sums/pallas_call | solution.py:72
  65.3 0.0 collective-permute-done.1.below_ref
  65.3 3.9 %collective-permute-done.above_ref = bf16[8,4,24,128]{3,2,1,0:T(8,128)(2,1)S(1)} collective-permute-done((bf16[8,4,24,128]{3,2,1,0:T(8,128)(2,1)S(1)}, bf16[8,4,24,128]{3,2,1,0:T(8,128)(2,1)S(1)}, u32[]{:S(2)}, u32[]{:S(2)}) %collective-permute-start) | collective-permute-done | bytes 196640 | tf_op jit(solution)/shard_map/ppermute | solution.py:238
  69.2 3.5 %act_block.1 = bf16[16,4,24,128]{3,2,1,0:T(8,128)(2,1)S(1)} custom-call(s32[6]{0:T(128)S(1)} %pad_add_fusion.flags_ref, bf16[16,4,24,128]{3,2,1,0:T(8,128)(2,1)S(1)} %all-to-all-done.1.own_ref, bf16[8,4,24,128]{3,2,1,0:T(8,128)(2,1)S(1)} %collective-permute-done.above_ref, bf16[8,4,24,128]{3,2,1,0:T(8,128)(2,1)S(1)} %collective-permute-done.1.below_ref, ...), custom_call_target="tpu_custom_call" | custom-call | flops 2000000000 | bytes 4000000 | tf_op jit(solution)/shard_map/act_block/pallas_call | solution.py:151
  72.8 18.0 %all_to_all.20 = bf16[16,4,24,128]{3,2,1,0:T(8,128)(2,1)} all-to-all(bf16[16,4,24,128]{3,2,1,0:T(8,128)(2,1)S(1)} %act_block.1), channel_id=1, replica_groups=mesh['sess'=16,'band'=32] {'sess'}, dimensions={0} | all-to-all | bytes 786432 | tf_op jit(solution)/shard_map/all_to_all | solution.py:204
  90.8 2.5 %to_homes.1 = bf16[64,24,128]{2,1,0:T(8,128)(2,1)} custom-call(s32[64]{0:T(128)} %map_ref.3, bf16[64,24,128]{2,1,0:T(8,128)(2,1)} %bitcast.47), custom_call_target="tpu_custom_call" | custom-call | tf_op jit(solution)/shard_map/to_homes/pallas_call | solution.py:195
  93.3 17.4 %all_to_all.21 = bf16[16,4,24,128]{3,2,1,0:T(8,128)(2,1)S(1)} all-to-all(bf16[16,4,24,128]{3,2,1,0:T(8,128)(2,1)} %bitcast.48), channel_id=1, replica_groups=mesh['sess'=16,'band'=32] {'sess'}, dimensions={0} | all-to-all | bytes 786432 | tf_op jit(solution)/shard_map/all_to_all | solution.py:204
  110.8 1.1 copy.47
  (19 shorter events, 0.1 us)
Async XLA Ops:
  0.0 9.7 %copy-start.1 = (bf16[4,2,2,96,4,128]{5,4,3,2,1,0:T(4,128)(2,1)S(1)}, bf16[4,2,2,96,4,128]{5,4,3,2,1,0:T(4,128)(2,1)}, u32[]{:S(2)}) copy-start(bf16[4,2,2,96,4,128]{5,4,3,2,1,0:T(4,128)(2,1)} %param.10) | copy-start | bytes 4718596
  1.9 28.1 %all-to-all-start = ((bf16[16,4,24,128]{3,2,1,0:T(8,128)(2,1)}), bf16[16,4,24,128]{3,2,1,0:T(8,128)(2,1)}, u32[]{:S(2)}, u32[]{:S(2)}) async-start(bf16[16,4,24,128]{3,2,1,0:T(8,128)(2,1)} %bitcast.4), calls=%async_computation | async-start | bytes 786432 | tf_op jit(solution)/shard_map/all_to_all | solution.py:204
  10.2 14.6 %copy-start.4 = (bf16[96,2592]{1,0:T(8,128)(2,1)S(1)}, bf16[96,2592]{1,0:T(8,128)(2,1)}, u32[]{:S(2)}) copy-start(bf16[96,2592]{1,0:T(8,128)(2,1)} %param.14) | copy-start | bytes 1492996
  11.1 33.1 %collective-permute-start.2 = (bf16[4,2,3,96,128]{4,3,1,0,2:T(8,128)(2,1)}, bf16[4,2,3,96,128]{4,3,1,0,2:T(8,128)(2,1)}, u32[]{:S(2)}, u32[]{:S(2)}) collective-permute-start(bf16[4,2,3,96,128]{4,3,1,0,2:T(8,128)(2,1)} %pad_maximum_fusion), channel_id=1, source_target_pairs={{0,1},{1,2},{2,3},{3,4},{4,5},{5,6},{6,7},{7,8},{8,9},{9,10},{10,1... | collective-permute-start | bytes 1769480 | tf_op jit(solution)/shard_map/ppermute | solution.py:227
  15.9 44.4 %collective-permute-start.3 = (bf16[4,2,3,96,128]{4,3,2,1,0:T(8,128)(2,1)}, bf16[4,2,3,96,128]{4,3,2,1,0:T(8,128)(2,1)}, u32[]{:S(2)}, u32[]{:S(2)}) collective-permute-start(bf16[4,2,3,96,128]{4,3,2,1,0:T(8,128)(2,1)} %pad_maximum_fusion.1), channel_id=1, source_target_pairs={{1,0},{2,1},{3,2},{4,3},{5,4},{6,5},{7,6},{8,7},{9,8},{10,9},{11,1... | collective-permute-start | bytes 1769480 | tf_op jit(solution)/shard_map/ppermute | solution.py:228
  29.9 10.3 %copy-start.5 = (s32[64]{0:T(128)S(1)}, s32[64]{0:T(128)}, u32[]{:S(2)}) copy-start(s32[64]{0:T(128)} %map_ref.3) | copy-start | bytes 772
  29.9 10.2 %copy-start.8 = (s32[64]{0:T(128)S(1)}, s32[64]{0:T(128)}, u32[]{:S(2)}) copy-start(s32[64]{0:T(128)} %param.12) | copy-start | bytes 772
  29.9 10.2 %copy-start.9 = (s32[64]{0:T(128)S(1)}, s32[64]{0:T(128)}, u32[]{:S(2)}) copy-start(s32[64]{0:T(128)} %param.13) | copy-start | bytes 772
  29.9 10.6 %copy-start.6 = (f32[96]{0:T(128)S(1)}, f32[96]{0:T(128)}, u32[]{:S(2)}) copy-start(f32[96]{0:T(128)} %param.16) | copy-start | bytes 1156
  29.9 10.7 %copy-start.7 = (f32[96]{0:T(128)S(1)}, f32[96]{0:T(128)}, u32[]{:S(2)}) copy-start(f32[96]{0:T(128)} %param.17) | copy-start | bytes 1156
  29.9 10.8 %copy-start.2 = (bf16[96,3,2,288]{0,3,2,1:T(8,128)(2,1)S(1)}, bf16[96,3,2,288]{0,3,2,1:T(8,128)(2,1)}, u32[]{:S(2)}) copy-start(bf16[96,3,2,288]{0,3,2,1:T(8,128)(2,1)} %slice.46) | copy-start | bytes 995332
  29.9 12.1 %copy-start.3 = (bf16[96,3,2,288]{0,3,2,1:T(8,128)(2,1)S(1)}, bf16[96,3,2,288]{0,3,2,1:T(8,128)(2,1)}, u32[]{:S(2)}) copy-start(bf16[96,3,2,288]{0,3,2,1:T(8,128)(2,1)} %slice.47) | copy-start | bytes 995332
  32.6 22.1 %all-to-all-start.1 = ((bf16[16,4,24,128]{3,2,1,0:T(8,128)(2,1)}), bf16[16,4,24,128]{3,2,1,0:T(8,128)(2,1)S(1)}, u32[]{:S(2)}, u32[]{:S(2)}) async-start(bf16[16,4,24,128]{3,2,1,0:T(8,128)(2,1)} %bitcast.46), calls=%async_computation.1 | async-start | bytes 786432 | tf_op jit(solution)/shard_map/all_to_all | solution.py:204
  54.7 10.6 %collective-permute-start.1 = (bf16[8,4,24,128]{3,2,1,0:T(8,128)(2,1)S(1)}, bf16[8,4,24,128]{3,2,1,0:T(8,128)(2,1)S(1)}, u32[]{:S(2)}, u32[]{:S(2)}) collective-permute-start(bf16[8,4,24,128]{3,2,1,0:T(8,128)(2,1)S(1)} %get-tuple-element.15), channel_id=1, source_target_pairs={{1,0},{2,1},{3,2},{4,3},{5,4},{6,5},{7,6},{8,7},{9,8},{10,9},{11,1... | collective-permute-start | bytes 589832 | tf_op jit(solution)/shard_map/ppermute | solution.py:239
  58.4 10.9 %collective-permute-start = (bf16[8,4,24,128]{3,2,1,0:T(8,128)(2,1)S(1)}, bf16[8,4,24,128]{3,2,1,0:T(8,128)(2,1)S(1)}, u32[]{:S(2)}, u32[]{:S(2)}) collective-permute-start(bf16[8,4,24,128]{3,2,1,0:T(8,128)(2,1)S(1)} %get-tuple-element.16), channel_id=1, source_target_pairs={{0,1},{1,2},{2,3},{3,4},{4,5},{5,6},{6,7},{7,8},{8,9},{9,10},{10,1... | collective-permute-start | bytes 589832 | tf_op jit(solution)/shard_map/ppermute | solution.py:238
  60.3 8.9 %copy-start = (bf16[96,864]{1,0:T(8,128)(2,1)S(1)}, bf16[96,864]{1,0:T(8,128)(2,1)}, u32[]{:S(2)}) copy-start(bf16[96,864]{1,0:T(8,128)(2,1)} %copy.44.w_two_ref) | copy-start | bytes 497668

commit v2 on v0

v2 whole, which is shorter than its diff:
```python
import functools

import jax
import jax.numpy as jnp
from jax import lax
from jax.experimental import pallas as pl
from jax.experimental.pallas import tpu as pltpu
from jax.sharding import PartitionSpec as P

F32 = jnp.float32
BF16 = jnp.bfloat16


def three_taps(values):
    width = values.shape[1]
    column = lax.broadcasted_iota(jnp.int32, values.shape, 1)
    before = jnp.where(column == 0, 0.0, pltpu.roll(values, 1, 1))
    after = jnp.where(column == width - 1, 0.0, pltpu.roll(values, width - 1, 1))
    return before.astype(BF16), values.astype(BF16), after.astype(BF16)


def store_taps(cols_ref, at, channels, half, values):
    width = values.shape[1]
    for tap, moved in enumerate(three_taps(values)):
        cols_ref[at + tap * channels : at + (tap + 1) * channels, half * width : (half + 1) * width] = moved


def norm_silu(values, gain):
    mean_square = jnp.mean(values * values, axis=0, keepdims=True)
    scaled = values * lax.rsqrt(mean_square + 1e-06) * gain
    return 0.5 * scaled * (1.0 + jnp.tanh(0.5 * scaled))


def past_kernel(place_ref, session_of_ref, counts_ref, own_ref, above_ref, below_ref, w_one_ref, w_two_ref, one_hbm, two_hbm, one_cols_ref, two_cols_ref, one_ref, two_ref, sems):
    _, rows, sessions, frames, channels, _ = own_ref.shape
    step = frames * 3 * channels
    copies = []
    for pair in range(sessions // 2):
        for half in range(2):
            session = 2 * pair + half
            count = counts_ref[session_of_ref[place_ref[0] * sessions + session]]
            for frame in range(frames):
                live = (frame >= 2 - count).astype(F32)
                one_rows = [above_ref.at[0], above_ref.at[1]] + [own_ref.at[0, r] for r in range(rows)] + [below_ref.at[0], below_ref.at[1]]
                two_rows = [above_ref.at[2]] + [own_ref.at[1, r] for r in range(rows)] + [below_ref.at[2]]
                for cols_ref, row_refs in ((one_cols_ref, one_rows), (two_cols_ref, two_rows)):
                    for slot, row_ref in enumerate(row_refs):
                        values = row_ref[session, frame].astype(F32) * live
                        store_taps(cols_ref.at[pair], slot * step + frame * 3 * channels, channels, half, values)
        for i, (out_hbm, out_ref, w_ref, cols_ref) in enumerate(
            ((one_hbm, one_ref, w_one_ref, one_cols_ref), (two_hbm, two_ref, w_two_ref, two_cols_ref))
        ):
            for row in range(out_ref.shape[1]):
                out_ref[pair, row] = jnp.dot(
                    w_ref[...], cols_ref[pair, row * step : (row + 3) * step, :], preferred_element_type=F32
                )
            copies.append(pltpu.make_async_copy(out_ref.at[pair], out_hbm.at[pair], sems.at[pair, i]))
            copies[-1].start()
    for copy in copies:
        copy.wait()


def past_sums(place, session_of, counts, own, above, below, w_one, w_two):
    _, rows, sessions, frames, channels, width = own.shape
    pairs, lanes, step = sessions // 2, 2 * width, frames * 3 * channels
    vmem, smem = pl.BlockSpec(memory_space=pltpu.VMEM), pl.BlockSpec(memory_space=pltpu.SMEM)
    return pl.pallas_call(
        past_kernel,
        in_specs=[smem, smem, smem, vmem, vmem, vmem, vmem, vmem],
        out_specs=[pl.BlockSpec(memory_space=pltpu.HBM)] * 2,
        out_shape=[
            pltpu.HBM((pairs, rows + 2, channels, lanes), F32),
            pltpu.HBM((pairs, rows, channels, lanes), F32),
        ],
        scratch_shapes=[
            pltpu.VMEM((pairs, (rows + 4) * step, lanes), BF16),
            pltpu.VMEM((pairs, (rows + 2) * step, lanes), BF16),
            pltpu.VMEM((pairs, rows + 2, channels, lanes), F32),
            pltpu.VMEM((pairs, rows, channels, lanes), F32),
            pltpu.SemaphoreType.DMA((pairs, 2)),
        ],
        compiler_params=pltpu.CompilerParams(vmem_limit_bytes=24 * 1024 * 1024),
        cost_estimate=pl.CostEstimate(flops=4 * 10**9, bytes_accessed=6 * 10**6, transcendentals=0),
        name="past_sums",
    )(place, session_of, counts, own, above, below, w_one, w_two)


def act_kernel(place_ref, session_of_ref, active_ref, own_ref, above_ref, below_ref, one_hbm, two_hbm, w_one_hbm, w_two_hbm, g_one_ref, g_two_ref, out_ref, cols_ref, acts_ref, one_ref, two_ref, w_one_ref, w_two_ref, sems, *, bands):
    channels, width = w_one_hbm.shape[0], own_ref.shape[3]
    sessions, part = own_ref.shape[1], own_ref.shape[2]
    parts = channels // part
    rows = own_ref.shape[0] // parts
    step = 3 * channels
    copies = [
        pltpu.make_async_copy(source, target, sems.at[i])
        for i, (source, target) in enumerate(
            ((w_one_hbm, w_one_ref), (one_hbm, one_ref), (w_two_hbm, w_two_ref), (two_hbm, two_ref))
        )
    ]
    for copy in copies:
        copy.start()
    first = (place_ref[1] > 0).astype(F32)
    last = (place_ref[1] < bands - 1).astype(F32)

    def frame_row(ref, row, session):
        return jnp.concatenate([ref[row * parts + q, session].astype(F32) for q in range(parts)], axis=0)

    g_one, g_two = g_one_ref[...], g_two_ref[...]
    for pair in range(sessions // 2):
        for slot in range(rows + 4):
            for half in range(2):
                if slot < 2:
                    values = frame_row(above_ref, slot, 2 * pair + half)
                elif slot < rows + 2:
                    values = frame_row(own_ref, slot - 2, 2 * pair + half)
                else:
                    values = frame_row(below_ref, slot - rows - 2, 2 * pair + half)
                store_taps(cols_ref.at[pair], slot * step, channels, half, norm_silu(values, g_one))
        if pair == 0:
            copies[0].wait()
            copies[1].wait()
        for row in range(rows + 2):
            hidden = one_ref[pair, row] + jnp.dot(
                w_one_ref[...], cols_ref[pair, row * step : (row + 3) * step, :], preferred_element_type=F32
            )
            act = norm_silu(hidden, g_two)
            if row == 0:
                act = act * first
            elif row == rows + 1:
                act = act * last
            for half in range(2):
                store_taps(acts_ref.at[pair], row * step, channels, half, act[:, half * width : (half + 1) * width])
        if pair == 0:
            copies[2].wait()
            copies[3].wait()
        for row in range(rows):
            hidden = two_ref[pair, row] + jnp.dot(
                w_two_ref[...], acts_ref[pair, row * step : (row + 3) * step, :], preferred_element_type=F32
            )
            for half in range(2):
                session = 2 * pair + half
                active = active_ref[session_of_ref[place_ref[0] * sessions + session]].astype(F32)
                total = active * (frame_row(own_ref, row, session) + hidden[:, half * width : (half + 1) * width])
                for q in range(parts):
                    out_ref[row * parts + q, session] = total[q * part : (q + 1) * part].astype(BF16)


def act_block(bands, place, session_of, active, own, above, below, one, two, w_one, w_two, g_one, g_two):
    pairs, rows, channels, lanes = two.shape
    step = 3 * channels
    one, two, w_one, w_two = (pltpu.with_memory_space_constraint(x, pltpu.HBM) for x in (one, two, w_one, w_two))
    vmem, smem = pl.BlockSpec(memory_space=pltpu.VMEM), pl.BlockSpec(memory_space=pltpu.SMEM)
    return pl.pallas_call(
        functools.partial(act_kernel, bands=bands),
        in_specs=[smem] * 3 + [vmem] * 3 + [pl.BlockSpec(memory_space=pltpu.HBM)] * 4 + [vmem] * 2,
        out_specs=vmem,
        out_shape=jax.ShapeDtypeStruct(own.shape, BF16),
        scratch_shapes=[
            pltpu.VMEM((pairs, (rows + 4) * step, lanes), BF16),
            pltpu.VMEM((pairs, (rows + 2) * step, lanes), BF16),
            pltpu.VMEM(one.shape, F32),
            pltpu.VMEM(two.shape, F32),
            pltpu.VMEM(w_one.shape, BF16),
            pltpu.VMEM(w_two.shape, BF16),
            pltpu.SemaphoreType.DMA((4,)),
        ],
        compiler_params=pltpu.CompilerParams(vmem_limit_bytes=20 * 1024 * 1024),
        cost_estimate=pl.CostEstimate(flops=2 * 10**9, bytes_accessed=4 * 10**6, transcendentals=10**6),
        name="act_block",
    )(place, session_of, active, own, above, below, one, two, w_one, w_two, g_one, g_two)


def weights_kernel(one_ref, two_ref, past_one_ref, past_two_ref, new_one_ref, new_two_ref):
    third = one_ref.shape[1] // 3
    new = third // 3
    past = third - new
    for source, past_out, new_out in ((one_ref, past_one_ref, new_one_ref), (two_ref, past_two_ref, new_two_ref)):
        values = source[...]
        rows = [values[:, dy * third : (dy + 1) * third] for dy in range(3)]
        past_out[...] = jnp.concatenate([row[:, :past] for row in rows], axis=1)
        new_out[...] = jnp.concatenate([row[:, past:] for row in rows], axis=1)


def split_weights(one, two):
    channels, columns = one.shape
    past = jax.ShapeDtypeStruct((channels, columns // 3 * 2), one.dtype)
    new = jax.ShapeDtypeStruct((channels, columns // 3), one.dtype)
    return pl.pallas_call(
        weights_kernel,
        out_shape=[past, past, new, new],
        compiler_params=pltpu.CompilerParams(vmem_limit_bytes=16 * 1024 * 1024),
        cost_estimate=pl.CostEstimate(flops=0, bytes_accessed=2 * 10**6, transcendentals=0),
        name="split_weights",
    )(one, two)


def take_slots(pieces, slots):
    return lax.gather(
        pieces,
        slots[:, None],
        lax.GatherDimensionNumbers(offset_dims=(1, 2), collapsed_slice_dims=(0,), start_index_map=(0,)),
        slice_sizes=(1,) + pieces.shape[1:],
        unique_indices=True,
        mode=lax.GatherScatterMode.CLIP,
    )


def take_kernel(slots_ref, in_ref, out_ref):
    for slot in range(in_ref.shape[0]):
        out_ref[slot] = in_ref[slots_ref[slot]]


def take_in_vmem(pieces, slots):
    vmem = pl.BlockSpec(memory_space=pltpu.VMEM)
    return pl.pallas_call(
        take_kernel,
        in_specs=[pl.BlockSpec(memory_space=pltpu.SMEM), vmem],
        out_specs=vmem,
        out_shape=jax.ShapeDtypeStruct(pieces.shape, pieces.dtype),
        compiler_params=pltpu.CompilerParams(vmem_limit_bytes=4 * 1024 * 1024),
        name="take_in_vmem",
    )(slots, pieces)


def exchange(pieces):
    return lax.all_to_all(pieces, "sess", 0, 0, tiled=True)


def local(frame, cache, holder_map, counts, active, weight_one, weight_two, gain_one, gain_two):
    sess_count, band_count = lax.axis_size("sess"), lax.axis_size("band")
    me, band = lax.axis_index("sess"), lax.axis_index("band")
    sessions, channels, rows, width = frame.shape
    parts = sess_count // rows
    part = channels // parts
    down = [(i, i + 1) for i in range(band_count - 1)]
    up = [(i + 1, i) for i in range(band_count - 1)]

    ids = jnp.arange(sess_count * sessions, dtype=jnp.int32)
    session_of = jnp.sum(jnp.where(holder_map[None, :] == ids[:, None], ids[None, :], 0), axis=1)
    place = jnp.stack([me, band]).astype(jnp.int32)

    cut = frame.reshape(sessions, parts, part, rows, width).transpose(3, 1, 0, 2, 4)
    cut, cache = lax.optimization_barrier((cut, cache))
    spread = exchange(cut.reshape(sess_count, sessions, part, width))

    own = cache.transpose(1, 4, 0, 2, 3, 5)
    above = lax.ppermute(jnp.concatenate([own[0, rows - 2 :], own[1, rows - 1 :]]), "band", down)
    below = lax.ppermute(jnp.concatenate([own[0, :2], own[1, :1]]), "band", up)
    past_one, past_two, new_one, new_two = split_weights(weight_one, weight_two)
    one, two = past_sums(place, session_of, counts, own, above, below, past_one, past_two)

    sorted_pieces = take_slots(spread.reshape(-1, part, width), session_of)
    held = exchange(sorted_pieces.reshape(sess_count, sessions, part, width))
    held, one, two = lax.optimization_barrier((held, one, two))
    half = sess_count - 2 * parts
    held_above = lax.ppermute(held[half:], "band", down)
    held_below = lax.ppermute(held[: 2 * parts], "band", up)
    result = act_block(
        band_count, place, session_of, active, held, held_above, held_below,
        one, two, new_one, new_two, gain_one[:, None], gain_two[:, None],
    )

    spread_result = exchange(result)
    home_pieces = take_in_vmem(spread_result.reshape(-1, part, width), holder_map)
    home = exchange(home_pieces.reshape(sess_count, sessions, part, width))
    home = home.reshape(rows, parts, sessions, part, width).transpose(2, 1, 3, 0, 4)
    return home.reshape(sessions, channels, rows, width)


def solution(mesh):
    return jax.shard_map(
        local,
        mesh=mesh,
        in_specs=(
            P("sess", None, "band", None),
            P("sess", None, None, None, "band", None),
            P(),
            P(),
            P(),
            P(),
            P(),
            P(),
            P(),
        ),
        out_specs=P("sess", None, "band", None),
        check_vma=False,
    )
```

time: 228 us -> 102 us (0.45)
  waiting for transfers between devices: 147 us -> 12 us
  blocking collectives: 0 us -> 34.6 us
  local copies, waits for them, and re-layouts: 24.9 us -> 6.43 us
  other arithmetic: 18.7 us -> 1.97 us
  Pallas kernels: 0 us -> 10.3 us
  starting transfers between devices: 29.3 us -> 35.8 us
  matrix products: 4.72 us -> 0 us
    all_to_all x1 -> x2, waiting for transfers between devices: 138 us -> 5.25 us  [exchange(): return lax.all_to_all(pieces, 'sess', 0, 0, tiled=True)]
    all_to_all x0 -> x2, blocking collectives: none -> 34.6 us  [exchange(): return lax.all_to_all(pieces, 'sess', 0, 0, tiled=True)]
    pallas_call x0 -> x4, Pallas kernels: none -> 10.3 us  [the longest x1 5.32 us: past_sums(): pl.pallas_call(past_kernel, in_specs=[smem, smem, smem, vmem, vmem, vmem,...]
    gather x2 -> x1, local copies, waits for them, and re-layouts: 11 us -> 1.38 us  [take_slots(): lax.gather(pieces, slots[:, None], lax.GatherDimensionNumbers(offset_dims...]
    select_n x5 -> x0, other arithmetic: 8.73 us -> none  [the longest x1 8.48 us: pack_slots(): jnp.where(filled.reshape((-1,) + tail_ones), picked, jnp.zeros_like(picked))]
    all_to_all x1 -> x2, starting transfers between devices: 7.93 us -> 15.3 us  [exchange(): return lax.all_to_all(pieces, 'sess', 0, 0, tiled=True)]
    all_to_all x1 -> x0, local copies, waits for them, and re-layouts: 7.14 us -> none  [local(): lax.all_to_all(outgoing, 'sess', split_axis=0, concat_axis=0, tiled=True)]
    dot_general x6 -> x0, matrix products: 4.72 us -> none  [causal_conv(): jnp.einsum('ok,skrw->sorw', weight_block, columns, preferred_element_type...]
  transfers between devices with their start and end apart: 5 -> 6, of which waited for: 5 -> 5; matrix products, arithmetic and copies ran while one was open for 0% -> 4% of each run, Pallas kernels for 0% -> 6%
where the time goes in v2:
time: 102 us; the launch traced here: 101 us
  starting transfers between devices  35.8 us (35%)
  blocking collectives  34.6 us (34%)
  waiting for transfers between devices  12 us (12%)
  Pallas kernels  10.3 us (10%)
  local copies, waits for them, and re-layouts  6.43 us (6%)
  other arithmetic  1.97 us (2%)
    all_to_all x2, blocking collectives, exchange(): return lax.all_to_all(pieces, 'sess', 0, 0, tiled=True)  34.6 us
    all_to_all x2, starting transfers between devices, exchange(): return lax.all_to_all(pieces, 'sess', 0, 0, tiled=True)  15.3 us
    ppermute x1, starting transfers between devices, local(): below = lax.ppermute(jnp.concatenate([own[0, :2], own[1, :1]]), 'band', up)  8.97 us
    ppermute x1, starting transfers between devices, local(): held_below = lax.ppermute(held[:2 * parts], 'band', up)  5.47 us
    pallas_call x1, Pallas kernels, past_sums(): pl.pallas_call(past_kernel, in_specs=[smem, smem, smem, vmem, vmem, vmem,...  5.32 us
    all_to_all x2, waiting for transfers between devices, exchange(): return lax.all_to_all(pieces, 'sess', 0, 0, tiled=True)  5.25 us
    pallas_call x1, Pallas kernels, act_block(): pl.pallas_call(functools.partial(act_kernel, bands=bands), in_specs=[smem...  4.15 us
    ppermute x1, starting transfers between devices, local(): lax.ppermute(jnp.concatenate([own[0, rows - 2:], own[1, rows - 1:]]), 'ba...  4.14 us
  transfers between devices with their start and end apart: 6, of which 5 were waited for; matrix products, arithmetic and copies ran while one was open for 4% of the time, Pallas kernels for 6%

profile of v2, /device:TPU:7, one launch (start us, length us, event | category | flops | bytes accessed | tf_op | source)
XLA Modules:
  0.0 101.2 jit_solution(8498704393690796578)
XLA Ops:
  0.0 0.0 copy-start.7
  0.0 1.2 %copy.24 = bf16[4,96,4,128]{3,1,2,0:T(8,128)(2,1)S(1)} copy(bf16[4,96,4,128]{3,2,1,0:T(4,128)(2,1)} %param.9) | data formatting | bytes 786432 | tf_op args[0]
  1.2 0.8 copy.25
  2.0 7.8 %all-to-all-start = ((bf16[16,4,24,128]{3,2,1,0:T(8,128)(2,1)}), bf16[16,4,24,128]{3,2,1,0:T(8,128)(2,1)S(1)}, u32[]{:S(2)}, u32[]{:S(2)}) async-start(bf16[16,4,24,128]{3,2,1,0:T(8,128)(2,1)} %bitcast.4), calls=%async_computation | async-start | bytes 786432 | tf_op jit(solution)/shard_map/all_to_all | solution.py:226
  9.8 0.0 copy-done.7
  9.8 0.4 copy.31
  10.2 0.1 slice_bitcast_fusion
  10.2 0.0 copy-start.2
  10.2 0.9 pad_maximum_fusion
  11.1 0.0 copy-start
  11.1 0.0 copy-start.1
  11.1 4.1 %collective-permute-start = (bf16[3,4,2,96,128]{4,3,2,1,0:T(8,128)(2,1)}, bf16[3,4,2,96,128]{4,3,2,1,0:T(8,128)(2,1)}, u32[]{:S(2)}, u32[]{:S(2)}) collective-permute-start(bf16[3,4,2,96,128]{4,3,2,1,0:T(8,128)(2,1)} %pad_maximum_fusion), channel_id=1, source_target_pairs={{0,1},{1,2},{2,3},{3,4},{4,5},{5,6},{6,7},{7,8},{8,9},{9,10},{10,1... | collective-permute-start | bytes 1769480 | tf_op jit(solution)/shard_map/ppermute | solution.py:247
  15.3 0.9 pad_maximum_fusion.1
  16.2 0.0 copy-start.5
  16.2 9.0 %collective-permute-start.1 = (bf16[3,4,2,96,128]{4,3,2,1,0:T(8,128)(2,1)}, bf16[3,4,2,96,128]{4,3,2,1,0:T(8,128)(2,1)}, u32[]{:S(2)}, u32[]{:S(2)}) collective-permute-start(bf16[3,4,2,96,128]{4,3,2,1,0:T(8,128)(2,1)} %pad_maximum_fusion.1), channel_id=1, source_target_pairs={{1,0},{2,1},{3,2},{4,3},{5,4},{6,5},{7,6},{8,7},{9,8},{10,9},{11,1... | collective-permute-start | bytes 1769480 | tf_op jit(solution)/shard_map/ppermute | solution.py:248
  25.2 0.0 copy-done.2
  25.2 0.1 select_reduce_fusion.session_of_ref
  25.3 0.0 all-to-all-done
  25.3 1.4 %gather_fusion = bf16[64,24,128]{2,1,0:T(8,128)(2,1)} fusion(bf16[64,24,128]{2,1,0:T(8,128)(2,1)S(1)} %bitcast.34, s32[1024]{0:T(1024)S(1)} %pad_clamp_fusion), kind=kCustom, calls=%fused_computation | custom fusion | bytes 786688 | tf_op jit(solution)/shard_map/gather | solution.py:198
  26.7 7.5 %all-to-all-start.1 = ((bf16[16,4,24,128]{3,2,1,0:T(8,128)(2,1)}), bf16[16,4,24,128]{3,2,1,0:T(8,128)(2,1)S(1)}, u32[]{:S(2)}, u32[]{:S(2)}) async-start(bf16[16,4,24,128]{3,2,1,0:T(8,128)(2,1)} %bitcast.6), calls=%async_computation.1 | async-start | bytes 786432 | tf_op jit(solution)/shard_map/all_to_all | solution.py:226
  34.2 0.0 copy-done
  34.2 0.0 copy-done.1
  34.2 0.3 split_weights.1
  34.5 0.0 copy-start.3
  34.5 0.7 copy-done.3
  35.1 0.0 copy-start.4
  35.1 0.7 copy-done.4
  35.8 0.1 pad_add_fusion.place_ref
  35.9 0.2 collective-permute-done.above_ref
  36.1 2.0 %collective-permute-done.1.below_ref = bf16[3,4,2,96,128]{4,3,2,1,0:T(8,128)(2,1)} collective-permute-done((bf16[3,4,2,96,128]{4,3,2,1,0:T(8,128)(2,1)}, bf16[3,4,2,96,128]{4,3,2,1,0:T(8,128)(2,1)}, u32[]{:S(2)}, u32[]{:S(2)}) %collective-permute-start.1) | collective-permute-done | bytes 589856 | tf_op jit(solution)/shard_map/ppermute | solution.py:248
  38.1 0.0 copy-done.5
  38.1 0.0 copy-start.8
  38.1 5.3 %past_sums.1 = (f32[2,6,96,256]{3,2,1,0:T(8,128)}, f32[2,4,96,256]{3,2,1,0:T(8,128)}) custom-call(s32[2]{0:T(128)S(1)} %pad_add_fusion.place_ref, s32[64]{0:T(128)S(1)} %select_reduce_fusion.session_of_ref, s32[64]{0:T(128)S(1)} %copy-done.5, bf16[2,4,4,2,96,128]{5,4,3,2,1,0:T(8,128)(2,1)S(1)} %bitcast.29, ...), custom_call_target="tpu_custom_call" | custom-call | flops 4000000000 | bytes 6000000 | tf_op jit(solution)/shard_map/past_sums/pallas_call | solution.py:67
  43.5 5.3 %all-to-all-done.1.own_ref = bf16[16,4,24,128]{3,2,1,0:T(8,128)(2,1)S(1)} async-done(((bf16[16,4,24,128]{3,2,1,0:T(8,128)(2,1)}), bf16[16,4,24,128]{3,2,1,0:T(8,128)(2,1)S(1)}, u32[]{:S(2)}, u32[]{:S(2)}) %all-to-all-start.1) | async-done | bytes 393248 | tf_op jit(solution)/shard_map/all_to_all | solution.py:226
  48.8 1.9 %collective-permute-start.2 = (bf16[8,4,24,128]{3,2,1,0:T(8,128)(2,1)S(1)}, bf16[8,4,24,128]{3,2,1,0:T(8,128)(2,1)S(1)}, u32[]{:S(2)}, u32[]{:S(2)}) collective-permute-start(bf16[8,4,24,128]{3,2,1,0:T(8,128)(2,1)S(1)} %get-tuple-element.32), channel_id=1, source_target_pairs={{0,1},{1,2},{2,3},{3,4},{4,5},{5,6},{6,7},{7,8},{8,9},{9,10},{10,1... | collective-permute-start | bytes 589832 | tf_op jit(solution)/shard_map/ppermute | solution.py:256
  50.7 5.5 %collective-permute-start.3 = (bf16[8,4,24,128]{3,2,1,0:T(8,128)(2,1)S(1)}, bf16[8,4,24,128]{3,2,1,0:T(8,128)(2,1)S(1)}, u32[]{:S(2)}, u32[]{:S(2)}) collective-permute-start(bf16[8,4,24,128]{3,2,1,0:T(8,128)(2,1)S(1)} %get-tuple-element.31), channel_id=1, source_target_pairs={{1,0},{2,1},{3,2},{4,3},{5,4},{6,5},{7,6},{8,7},{9,8},{10,9},{11,1... | collective-permute-start | bytes 589832 | tf_op jit(solution)/shard_map/ppermute | solution.py:257
  56.2 0.0 copy-done.8
  56.2 0.1 copy.27.g_one_ref
  56.3 0.0 copy-done.9
  56.3 0.1 copy.28.g_two_ref
  56.4 2.7 %collective-permute-done.2.above_ref = bf16[8,4,24,128]{3,2,1,0:T(8,128)(2,1)S(1)} collective-permute-done((bf16[8,4,24,128]{3,2,1,0:T(8,128)(2,1)S(1)}, bf16[8,4,24,128]{3,2,1,0:T(8,128)(2,1)S(1)}, u32[]{:S(2)}, u32[]{:S(2)}) %collective-permute-start.2) | collective-permute-done | bytes 196640 | tf_op jit(solution)/shard_map/ppermute | solution.py:256
  59.1 1.8 %collective-permute-done.3.below_ref = bf16[8,4,24,128]{3,2,1,0:T(8,128)(2,1)S(1)} collective-permute-done((bf16[8,4,24,128]{3,2,1,0:T(8,128)(2,1)S(1)}, bf16[8,4,24,128]{3,2,1,0:T(8,128)(2,1)S(1)}, u32[]{:S(2)}, u32[]{:S(2)}) %collective-permute-start.3) | collective-permute-done | bytes 196640 | tf_op jit(solution)/shard_map/ppermute | solution.py:257
  60.9 0.0 copy-done.6
  60.9 4.1 %act_block.1 = bf16[16,4,24,128]{3,2,1,0:T(8,128)(2,1)S(1)} custom-call(s32[2]{0:T(128)S(1)} %pad_add_fusion.place_ref, s32[64]{0:T(128)S(1)} %select_reduce_fusion.session_of_ref, s32[64]{0:T(128)S(1)} %copy-done.6, bf16[16,4,24,128]{3,2,1,0:T(8,128)(2,1)S(1)} %all-to-all-done.1.own_ref, bf16[8,4,24,128]{3,2,1,0:T(8,128)(2,1)S(1)} %collective-permute-done.2.above_ref, ...), custom_call_target="tpu_custom_call" | custom-call | flops 2000000000 | bytes 4000000 | tf_op jit(solution)/shard_map/act_block/pallas_call | solution.py:153
  65.0 17.3 %all_to_all.20 = bf16[16,4,24,128]{3,2,1,0:T(8,128)(2,1)S(1)} all-to-all(bf16[16,4,24,128]{3,2,1,0:T(8,128)(2,1)S(1)} %act_block.1), channel_id=1, replica_groups=mesh['sess'=16,'band'=32] {'sess'}, dimensions={0} | all-to-all | bytes 786432 | tf_op jit(solution)/shard_map/all_to_all | solution.py:226
  82.3 0.6 take_in_vmem.1
  82.9 17.3 %all_to_all.21 = bf16[16,4,24,128]{3,2,1,0:T(8,128)(2,1)S(1)} all-to-all(bf16[16,4,24,128]{3,2,1,0:T(8,128)(2,1)S(1)} %bitcast.31), channel_id=1, replica_groups=mesh['sess'=16,'band'=32] {'sess'}, dimensions={0} | all-to-all | bytes 786432 | tf_op jit(solution)/shard_map/all_to_all | solution.py:226
  100.2 1.1 %copy.29 = bf16[4,4,4,24,128]{4,0,3,1,2:T(4,128)(2,1)} copy(bf16[4,4,4,24,128]{4,3,2,1,0:T(8,128)(2,1)S(1)} %bitcast.32) | data formatting | bytes 786432 | tf_op jit(solution)/shard_map/reshape | solution.py:266
  (5 shorter events, 0.1 us)
Async XLA Ops:
  0.0 9.8 %copy-start.7 = (bf16[4,2,2,96,4,128]{5,4,3,2,1,0:T(4,128)(2,1)S(1)}, bf16[4,2,2,96,4,128]{5,4,3,2,1,0:T(4,128)(2,1)}, u32[]{:S(2)}) copy-start(bf16[4,2,2,96,4,128]{5,4,3,2,1,0:T(4,128)(2,1)} %param.10) | copy-start | bytes 4718596
  2.0 23.3 %all-to-all-start = ((bf16[16,4,24,128]{3,2,1,0:T(8,128)(2,1)}), bf16[16,4,24,128]{3,2,1,0:T(8,128)(2,1)S(1)}, u32[]{:S(2)}, u32[]{:S(2)}) async-start(bf16[16,4,24,128]{3,2,1,0:T(8,128)(2,1)} %bitcast.4), calls=%async_computation | async-start | bytes 786432 | tf_op jit(solution)/shard_map/all_to_all | solution.py:226
  10.2 14.9 %copy-start.2 = (s32[64]{0:T(128)S(1)}, s32[64]{0:T(128)}, u32[]{:S(2)}) copy-start(s32[64]{0:T(128)} %slots_ref.1) | copy-start | bytes 772
  11.1 23.0 %copy-start = (bf16[96,2592]{1,0:T(8,128)(2,1)S(1)}, bf16[96,2592]{1,0:T(8,128)(2,1)}, u32[]{:S(2)}) copy-start(bf16[96,2592]{1,0:T(8,128)(2,1)} %one_ref.1) | copy-start | bytes 1492996
  11.1 23.0 %copy-start.1 = (bf16[96,2592]{1,0:T(8,128)(2,1)S(1)}, bf16[96,2592]{1,0:T(8,128)(2,1)}, u32[]{:S(2)}) copy-start(bf16[96,2592]{1,0:T(8,128)(2,1)} %two_ref.1) | copy-start | bytes 1492996
  11.1 25.0 %collective-permute-start = (bf16[3,4,2,96,128]{4,3,2,1,0:T(8,128)(2,1)}, bf16[3,4,2,96,128]{4,3,2,1,0:T(8,128)(2,1)}, u32[]{:S(2)}, u32[]{:S(2)}) collective-permute-start(bf16[3,4,2,96,128]{4,3,2,1,0:T(8,128)(2,1)} %pad_maximum_fusion), channel_id=1, source_target_pairs={{0,1},{1,2},{2,3},{3,4},{4,5},{5,6},{6,7},{7,8},{8,9},{9,10},{10,1... | collective-permute-start | bytes 1769480 | tf_op jit(solution)/shard_map/ppermute | solution.py:247
  16.2 22.0 %copy-start.5 = (s32[64]{0:T(128)S(1)}, s32[64]{0:T(128)}, u32[]{:S(2)}) copy-start(s32[64]{0:T(128)} %counts_ref.1) | copy-start | bytes 772
  16.2 21.9 %collective-permute-start.1 = (bf16[3,4,2,96,128]{4,3,2,1,0:T(8,128)(2,1)}, bf16[3,4,2,96,128]{4,3,2,1,0:T(8,128)(2,1)}, u32[]{:S(2)}, u32[]{:S(2)}) collective-permute-start(bf16[3,4,2,96,128]{4,3,2,1,0:T(8,128)(2,1)} %pad_maximum_fusion.1), channel_id=1, source_target_pairs={{1,0},{2,1},{3,2},{4,3},{5,4},{6,5},{7,6},{8,7},{9,8},{10,9},{11,1... | collective-permute-start | bytes 1769480 | tf_op jit(solution)/shard_map/ppermute | solution.py:248
  26.7 22.0 %all-to-all-start.1 = ((bf16[16,4,24,128]{3,2,1,0:T(8,128)(2,1)}), bf16[16,4,24,128]{3,2,1,0:T(8,128)(2,1)S(1)}, u32[]{:S(2)}, u32[]{:S(2)}) async-start(bf16[16,4,24,128]{3,2,1,0:T(8,128)(2,1)} %bitcast.6), calls=%async_computation.1 | async-start | bytes 786432 | tf_op jit(solution)/shard_map/all_to_all | solution.py:226
  34.5 0.7 copy-start.3
  35.1 0.7 copy-start.4
  38.1 18.0 %copy-start.8 = (f32[96]{0:T(128)S(1)}, f32[96]{0:T(128)}, u32[]{:S(2)}) copy-start(f32[96]{0:T(128)} %param.16) | copy-start | bytes 1156
  38.1 18.2 %copy-start.9 = (f32[96]{0:T(128)S(1)}, f32[96]{0:T(128)}, u32[]{:S(2)}) copy-start(f32[96]{0:T(128)} %param.17) | copy-start | bytes 1156
  38.1 22.7 %copy-start.6 = (s32[64]{0:T(128)S(1)}, s32[64]{0:T(128)}, u32[]{:S(2)}) copy-start(s32[64]{0:T(128)} %active_ref.1) | copy-start | bytes 772
  48.8 10.3 %collective-permute-start.2 = (bf16[8,4,24,128]{3,2,1,0:T(8,128)(2,1)S(1)}, bf16[8,4,24,128]{3,2,1,0:T(8,128)(2,1)S(1)}, u32[]{:S(2)}, u32[]{:S(2)}) collective-permute-start(bf16[8,4,24,128]{3,2,1,0:T(8,128)(2,1)S(1)} %get-tuple-element.32), channel_id=1, source_target_pairs={{0,1},{1,2},{2,3},{3,4},{4,5},{5,6},{6,7},{7,8},{8,9},{9,10},{10,1... | collective-permute-start | bytes 589832 | tf_op jit(solution)/shard_map/ppermute | solution.py:256
  50.7 10.2 %collective-permute-start.3 = (bf16[8,4,24,128]{3,2,1,0:T(8,128)(2,1)S(1)}, bf16[8,4,24,128]{3,2,1,0:T(8,128)(2,1)S(1)}, u32[]{:S(2)}, u32[]{:S(2)}) collective-permute-start(bf16[8,4,24,128]{3,2,1,0:T(8,128)(2,1)S(1)} %get-tuple-element.31), channel_id=1, source_target_pairs={{1,0},{2,1},{3,2},{4,3},{5,4},{6,5},{7,6},{8,7},{9,8},{10,9},{11,1... | collective-permute-start | bytes 589832 | tf_op jit(solution)/shard_map/ppermute | solution.py:257

commit v3 on v2

--- a/solution.py
+++ b/solution.py
@@ -31,7 +31,7 @@
     return 0.5 * scaled * (1.0 + jnp.tanh(0.5 * scaled))
 
 
-def past_kernel(place_ref, session_of_ref, counts_ref, own_ref, above_ref, below_ref, w_one_ref, w_two_ref, one_hbm, two_hbm, one_cols_ref, two_cols_ref, one_ref, two_ref, sems):
+def past_kernel(place_ref, session_of_ref, counts_ref, own_ref, below_ref, above_ref, w_one_ref, w_two_ref, one_hbm, two_hbm, one_cols_ref, two_cols_ref, one_ref, two_ref, sems):
     _, rows, sessions, frames, channels, _ = own_ref.shape
     step = frames * 3 * channels
     copies = []
@@ -82,92 +82,138 @@
         compiler_params=pltpu.CompilerParams(vmem_limit_bytes=24 * 1024 * 1024),
         cost_estimate=pl.CostEstimate(flops=4 * 10**9, bytes_accessed=6 * 10**6, transcendentals=0),
         name="past_sums",
-    )(place, session_of, counts, own, above, below, w_one, w_two)
-
-
-def act_kernel(place_ref, session_of_ref, active_ref, own_ref, above_ref, below_ref, one_hbm, two_hbm, w_one_hbm, w_two_hbm, g_one_ref, g_two_ref, out_ref, cols_ref, acts_ref, one_ref, two_ref, w_one_ref, w_two_ref, sems, *, bands):
-    channels, width = w_one_hbm.shape[0], own_ref.shape[3]
-    sessions, part = own_ref.shape[1], own_ref.shape[2]
-    parts = channels // part
+    )(place, session_of, counts, own, below, above, w_one, w_two)
+
+
+def frame_row(ref, row, session, parts):
+    return jnp.concatenate([ref[row * parts + q, session].astype(F32) for q in range(parts)], axis=0)
+
+
+def store_act(cols_ref, pair, slot, act):
+    channels, width = act.shape[0], act.shape[1] // 2
+    for half in range(2):
+        store_taps(cols_ref.at[pair], slot * 3 * channels, channels, half, act[:, half * width : (half + 1) * width])
+
+
+def own_kernel(own_ref, one_hbm, two_hbm, w_one_hbm, w_two_hbm, g_one_ref, g_two_ref, cols_ref, acts_ref, one_ref, two_ref, w_one_ref, w_two_ref, sems):
+    channels = w_one_hbm.shape[0]
+    parts = channels // own_ref.shape[2]
     rows = own_ref.shape[0] // parts
     step = 3 * channels
     copies = [
         pltpu.make_async_copy(source, target, sems.at[i])
         for i, (source, target) in enumerate(
-            ((w_one_hbm, w_one_ref), (one_hbm, one_ref), (w_two_hbm, w_two_ref), (two_hbm, two_ref))
+            ((w_one_hbm, w_one_ref), (one_hbm, one_ref), (two_hbm, two_ref), (w_two_hbm, w_two_ref))
         )
     ]
     for copy in copies:
         copy.start()
-    first = (place_ref[1] > 0).astype(F32)
-    last = (place_ref[1] < bands - 1).astype(F32)
-
-    def frame_row(ref, row, session):
-        return jnp.concatenate([ref[row * parts + q, session].astype(F32) for q in range(parts)], axis=0)
-
     g_one, g_two = g_one_ref[...], g_two_ref[...]
+    pairs = own_ref.shape[1] // 2
+    for pair in range(pairs):
+        for row in range(rows):
+            for half in range(2):
+                act = norm_silu(frame_row(own_ref, row, 2 * pair + half, parts), g_one)
+                store_taps(cols_ref.at[pair], row * step, channels, half, act)
+    copies[0].wait()
+    copies[1].wait()
+    for pair in range(pairs):
+        for row in range(rows - 2):
+            hidden = one_ref[pair, row + 2] + jnp.dot(
+                w_one_ref[...], cols_ref[pair, row * step : (row + 3) * step, :], preferred_element_type=F32
+            )
+            store_act(acts_ref, pair, row, norm_silu(hidden, g_two))
+    copies[2].wait()
+    copies[3].wait()
+
+
+def own_rows(own, one, two, w_one, w_two, g_one, g_two):
+    pairs, rows, channels, lanes = two.shape
+    step = 3 * channels
+    vmem, hbm = pl.BlockSpec(memory_space=pltpu.VMEM), pl.BlockSpec(memory_space=pltpu.HBM)
+    one, two, w_one, w_two = (pltpu.with_memory_space_constraint(x, pltpu.HBM) for x in (one, two, w_one, w_two))
+    return pl.pallas_call(
+        own_kernel,
+        in_specs=[vmem] + [hbm] * 4 + [vmem] * 2,
+        out_specs=[vmem] * 6,
+        out_shape=[
+            jax.ShapeDtypeStruct((pairs, rows * step, lanes), BF16),
+            jax.ShapeDtypeStruct((pairs, (rows - 2) * step, lanes), BF16),
+            jax.ShapeDtypeStruct(one.shape, F32),
+            jax.ShapeDtypeStruct(two.shape, F32),
+            jax.ShapeDtypeStruct(w_one.shape, BF16),
+            jax.ShapeDtypeStruct(w_two.shape, BF16),
+        ],
+        scratch_shapes=[pltpu.SemaphoreType.DMA((4,))],
+        compiler_params=pltpu.CompilerParams(vmem_limit_bytes=16 * 1024 * 1024),
+        cost_estimate=pl.CostEstimate(flops=10**9, bytes_accessed=4 * 10**6, transcendentals=10**6),
+        name="own_rows",
+    )(own, one, two, w_one, w_two, g_one, g_two)
+
+
+def side_kernel(place_ref, session_of_ref, active_ref, halo_ref, own_ref, own_cols_ref, mid_acts_ref, one_ref, two_ref, w_one_ref, w_two_ref, g_one_ref, g_two_ref, *rest, top, bands):
+    out_ref, cols_ref, acts_ref = rest[-3:]
+    channels = w_one_ref.shape[0]
+    sessions, part = own_ref.shape[1], own_ref.shape[2]
+    width = own_ref.shape[3]
+    parts = channels // part
+    rows = own_ref.shape[0] // parts
+    step = 3 * channels
+    inside = ((place_ref[1] > 0) if top else (place_ref[1] < bands - 1)).astype(F32)
+    g_one, g_two = g_one_ref[...], g_two_ref[...]
+    halo_at, own_at = (0, 2) if top else (2, 0)
     for pair in range(sessions // 2):
-        for slot in range(rows + 4):
+        for row in range(2):
             for half in range(2):
-                if slot < 2:
-                    values = frame_row(above_ref, slot, 2 * pair + half)
-                elif slot < rows + 2:
-                    values = frame_row(own_ref, slot - 2, 2 * pair + half)
-                else:
-                    values = frame_row(below_ref, slot - rows - 2, 2 * pair + half)
-                store_taps(cols_ref.at[pair], slot * step, channels, half, norm_silu(values, g_one))
-        if pair == 0:
-            copies[0].wait()
-            copies[1].wait()
-        for row in range(rows + 2):
-            hidden = one_ref[pair, row] + jnp.dot(
+                act = norm_silu(frame_row(halo_ref, row, 2 * pair + half, parts), g_one)
+                store_taps(cols_ref.at[pair], (halo_at + row) * step, channels, half, act)
+        from_row = 0 if top else rows - 2
+        cols_ref[pair, own_at * step : (own_at + 2) * step, :] = own_cols_ref[pair, from_row * step : (from_row + 2) * step, :]
+        acts_ref[pair, own_at * step : (own_at + 2) * step, :] = mid_acts_ref[pair]
+    first = 0 if top else rows
+    for pair in range(sessions // 2):
+        for row in range(2):
+            hidden = one_ref[pair, first + row] + jnp.dot(
                 w_one_ref[...], cols_ref[pair, row * step : (row + 3) * step, :], preferred_element_type=F32
             )
             act = norm_silu(hidden, g_two)
-            if row == 0:
-                act = act * first
-            elif row == rows + 1:
-                act = act * last
-            for half in range(2):
-                store_taps(acts_ref.at[pair], row * step, channels, half, act[:, half * width : (half + 1) * width])
-        if pair == 0:
-            copies[2].wait()
-            copies[3].wait()
-        for row in range(rows):
-            hidden = two_ref[pair, row] + jnp.dot(
+            if row == (0 if top else 1):
+                act = act * inside
+            store_act(acts_ref, pair, halo_at + row, act)
+    first = 0 if top else rows - 2
+    for pair in range(sessions // 2):
+        for row in range(2):
+            hidden = two_ref[pair, first + row] + jnp.dot(
                 w_two_ref[...], acts_ref[pair, row * step : (row + 3) * step, :], preferred_element_type=F32
             )
             for half in range(2):
                 session = 2 * pair + half
                 active = active_ref[session_of_ref[place_ref[0] * sessions + session]].astype(F32)
-                total = active * (frame_row(own_ref, row, session) + hidden[:, half * width : (half + 1) * width])
+                total = active * (
+                    frame_row(own_ref, first + row, session, parts) + hidden[:, half * width : (half + 1) * width]
+                )
                 for q in range(parts):
-                    out_ref[row * parts + q, session] = total[q * part : (q + 1) * part].astype(BF16)
-
-
-def act_block(bands, place, session_of, active, own, above, below, one, two, w_one, w_two, g_one, g_two):
+                    out_ref[(first + row) * parts + q, session] = total[q * part : (q + 1) * part].astype(BF16)
+
+
+def side_rows(top, bands, place, session_of, active, halo, own, held, g_one, g_two, earlier=None):
+    own_cols, mid_acts, one, two, w_one, w_two = held
     pairs, rows, channels, lanes = two.shape
     step = 3 * channels
-    one, two, w_one, w_two = (pltpu.with_memory_space_constraint(x, pltpu.HBM) for x in (one, two, w_one, w_two))
     vmem, smem = pl.BlockSpec(memory_space=pltpu.VMEM), pl.BlockSpec(memory_space=pltpu.SMEM)
-    return pl.pallas_call(
-        functools.partial(act_kernel, bands=bands),
-        in_specs=[smem] * 3 + [vmem] * 3 + [pl.BlockSpec(memory_space=pltpu.HBM)] * 4 + [vmem] * 2,
+    operands = [place, session_of, active, halo, own, own_cols, mid_acts, one, two, w_one, w_two, g_one, g_two]
+    operands += [] if earlier is None else [earlier]
+    return pl.pallas_call(
+        functools.partial(side_kernel, top=top, bands=bands),
+        in_specs=[smem] * 3 + [vmem] * (len(operands) - 3),
         out_specs=vmem,
         out_shape=jax.ShapeDtypeStruct(own.shape, BF16),
-        scratch_shapes=[
-            pltpu.VMEM((pairs, (rows + 4) * step, lanes), BF16),
-            pltpu.VMEM((pairs, (rows + 2) * step, lanes), BF16),
-            pltpu.VMEM(one.shape, F32),
-            pltpu.VMEM(two.shape, F32),
-            pltpu.VMEM(w_one.shape, BF16),
-            pltpu.VMEM(w_two.shape, BF16),
-            pltpu.SemaphoreType.DMA((4,)),
-        ],
-        compiler_params=pltpu.CompilerParams(vmem_limit_bytes=20 * 1024 * 1024),
-        cost_estimate=pl.CostEstimate(flops=2 * 10**9, bytes_accessed=4 * 10**6, transcendentals=10**6),
-        name="act_block",
-    )(place, session_of, active, own, above, below, one, two, w_one, w_two, g_one, g_two)
+        input_output_aliases={} if earlier is None else {len(operands) - 1: 0},
+        scratch_shapes=[pltpu.VMEM((pairs, 4 * step, lanes), BF16), pltpu.VMEM((pairs, 4 * step, lanes), BF16)],
+        compiler_params=pltpu.CompilerParams(vmem_limit_bytes=16 * 1024 * 1024),
+        cost_estimate=pl.CostEstimate(flops=10**9, bytes_accessed=4 * 10**6, transcendentals=10**6),
+        name="top_rows" if top else "bottom_rows",
+    )(*operands)
 
 
 def weights_kernel(one_ref, two_ref, past_one_ref, past_two_ref, new_one_ref, new_two_ref):
@@ -244,8 +290,8 @@
     spread = exchange(cut.reshape(sess_count, sessions, part, width))
 
     own = cache.transpose(1, 4, 0, 2, 3, 5)
+    below = lax.ppermute(jnp.concatenate([own[0, :2], own[1, :1]]), "band", up)
     above = lax.ppermute(jnp.concatenate([own[0, rows - 2 :], own[1, rows - 1 :]]), "band", down)
-    below = lax.ppermute(jnp.concatenate([own[0, :2], own[1, :1]]), "band", up)
     past_one, past_two, new_one, new_two = split_weights(weight_one, weight_two)
     one, two = past_sums(place, session_of, counts, own, above, below, past_one, past_two)
 
@@ -255,10 +301,10 @@
     half = sess_count - 2 * parts
     held_above = lax.ppermute(held[half:], "band", down)
     held_below = lax.ppermute(held[: 2 * parts], "band", up)
-    result = act_block(
-        band_count, place, session_of, active, held, held_above, held_below,
-        one, two, new_one, new_two, gain_one[:, None], gain_two[:, None],
-    )
+    gains = gain_one[:, None], gain_two[:, None]
+    inner = own_rows(held, one, two, new_one, new_two, *gains)
+    upper = side_rows(True, band_count, place, session_of, active, held_above, held, inner, *gains)
+    result = side_rows(False, band_count, place, session_of, active, held_below, held, inner, *gains, earlier=upper)
 
     spread_result = exchange(result)
     home_pieces = take_in_vmem(spread_result.reshape(-1, part, width), holder_map)

time: 102 us -> 99.6 us (0.976)
  waiting for transfers between devices: 12 us -> 8.2 us
  Pallas kernels: 10.3 us -> 11.5 us
    ppermute x1, waiting for transfers between devices: 2.69 us -> 0.64 us  [local(): held_above = lax.ppermute(held[half:], 'band', down)]
    ppermute x1, waiting for transfers between devices: 1.78 us -> 0.03 us  [local(): held_below = lax.ppermute(held[:2 * parts], 'band', up)]
    pallas_call x1 -> x3, Pallas kernels: 4.15 us -> 5.36 us  [the longest x2 3.33 us: side_rows(): pl.pallas_call(functools.partial(side_kernel, top=top, bands=bands), in_s...]
  transfers between devices with their start and end apart: 6 -> 6, of which waited for: 5 -> 4; matrix products, arithmetic and copies ran while one was open for 4% -> 4% of each run, Pallas kernels for 6% -> 9%
where the time goes in v3:
time: 99.6 us; the launch traced here: 99.1 us
  starting transfers between devices  35.8 us (36%)
  blocking collectives  35 us (35%)
  Pallas kernels  11.5 us (12%)
  waiting for transfers between devices  8.2 us (8%)
  local copies, waits for them, and re-layouts  6.44 us (6%)
  other arithmetic  1.96 us (2%)
    all_to_all x2, blocking collectives, exchange(): return lax.all_to_all(pieces, 'sess', 0, 0, tiled=True)  35 us
    all_to_all x2, starting transfers between devices, exchange(): return lax.all_to_all(pieces, 'sess', 0, 0, tiled=True)  15.3 us
    ppermute x1, starting transfers between devices, local(): below = lax.ppermute(jnp.concatenate([own[0, :2], own[1, :1]]), 'band', up)  8.97 us
    ppermute x1, starting transfers between devices, local(): held_below = lax.ppermute(held[:2 * parts], 'band', up)  5.47 us
    pallas_call x1, Pallas kernels, past_sums(): pl.pallas_call(past_kernel, in_specs=[smem, smem, smem, vmem, vmem, vmem,...  5.3 us
    all_to_all x2, waiting for transfers between devices, exchange(): return lax.all_to_all(pieces, 'sess', 0, 0, tiled=True)  5.28 us
    ppermute x1, starting transfers between devices, local(): lax.ppermute(jnp.concatenate([own[0, rows - 2:], own[1, rows - 1:]]), 'ba...  4.14 us
    pallas_call x2, Pallas kernels, side_rows(): pl.pallas_call(functools.partial(side_kernel, top=top, bands=bands), in_s...  3.33 us
  transfers between devices with their start and end apart: 6, of which 4 were waited for; matrix products, arithmetic and copies ran while one was open for 4% of the time, Pallas kernels for 9%

profile of v3, /device:TPU:7, one launch (start us, length us, event | category | flops | bytes accessed | tf_op | source)
XLA Modules:
  0.0 99.1 jit_solution(3908456165065848456)
XLA Ops:
  0.0 0.0 copy-start.7
  0.0 1.2 %copy.37 = bf16[4,96,4,128]{3,1,2,0:T(8,128)(2,1)S(1)} copy(bf16[4,96,4,128]{3,2,1,0:T(4,128)(2,1)} %param.9) | data formatting | bytes 786432 | tf_op args[0]
  1.2 0.8 copy.38
  2.0 7.8 %all-to-all-start = ((bf16[16,4,24,128]{3,2,1,0:T(8,128)(2,1)}), bf16[16,4,24,128]{3,2,1,0:T(8,128)(2,1)S(1)}, u32[]{:S(2)}, u32[]{:S(2)}) async-start(bf16[16,4,24,128]{3,2,1,0:T(8,128)(2,1)} %bitcast.4), calls=%async_computation | async-start | bytes 786432 | tf_op jit(solution)/shard_map/all_to_all | solution.py:272
  9.8 0.0 copy-done.7
  9.8 0.4 copy.48
  10.2 0.1 slice_bitcast_fusion
  10.2 0.0 copy-start.3
  10.2 0.9 pad_maximum_fusion.1
  11.1 0.0 copy-start
  11.1 0.0 copy-start.1
  11.1 4.1 %collective-permute-start.1 = (bf16[3,4,2,96,128]{4,3,2,1,0:T(8,128)(2,1)}, bf16[3,4,2,96,128]{4,3,2,1,0:T(8,128)(2,1)}, u32[]{:S(2)}, u32[]{:S(2)}) collective-permute-start(bf16[3,4,2,96,128]{4,3,2,1,0:T(8,128)(2,1)} %pad_maximum_fusion.1), channel_id=1, source_target_pairs={{0,1},{1,2},{2,3},{3,4},{4,5},{5,6},{6,7},{7,8},{8,9},{9,10},{10,1... | collective-permute-start | bytes 1769480 | tf_op jit(solution)/shard_map/ppermute | solution.py:294
  15.3 0.9 pad_maximum_fusion
  16.2 9.0 %collective-permute-start = (bf16[3,4,2,96,128]{4,3,2,1,0:T(8,128)(2,1)}, bf16[3,4,2,96,128]{4,3,2,1,0:T(8,128)(2,1)}, u32[]{:S(2)}, u32[]{:S(2)}) collective-permute-start(bf16[3,4,2,96,128]{4,3,2,1,0:T(8,128)(2,1)} %pad_maximum_fusion), channel_id=1, source_target_pairs={{1,0},{2,1},{3,2},{4,3},{5,4},{6,5},{7,6},{8,7},{9,8},{10,9},{11,1... | collective-permute-start | bytes 1769480 | tf_op jit(solution)/shard_map/ppermute | solution.py:293
  25.2 0.0 copy-done.3
  25.2 0.1 select_reduce_fusion.session_of_ref
  25.3 0.0 all-to-all-done
  25.3 1.4 %gather_fusion = bf16[64,24,128]{2,1,0:T(8,128)(2,1)} fusion(bf16[64,24,128]{2,1,0:T(8,128)(2,1)S(1)} %bitcast.34, s32[1024]{0:T(1024)S(1)} %pad_clamp_fusion), kind=kCustom, calls=%fused_computation | custom fusion | bytes 786688 | tf_op jit(solution)/shard_map/gather | solution.py:244
  26.7 7.5 %all-to-all-start.1 = ((bf16[16,4,24,128]{3,2,1,0:T(8,128)(2,1)}), bf16[16,4,24,128]{3,2,1,0:T(8,128)(2,1)S(1)}, u32[]{:S(2)}, u32[]{:S(2)}) async-start(bf16[16,4,24,128]{3,2,1,0:T(8,128)(2,1)} %bitcast.6), calls=%async_computation.1 | async-start | bytes 786432 | tf_op jit(solution)/shard_map/all_to_all | solution.py:272
  34.2 0.0 copy-done
  34.2 0.0 copy-done.1
  34.2 0.3 split_weights.1
  34.5 0.0 copy-start.4
  34.5 0.6 copy-done.4
  35.1 0.0 copy-start.5
  35.1 0.7 copy-done.5
  35.8 0.1 pad_add_fusion.place_ref
  35.9 0.2 collective-permute-done.1.above_ref
  36.1 2.0 %collective-permute-done.below_ref = bf16[3,4,2,96,128]{4,3,2,1,0:T(8,128)(2,1)} collective-permute-done((bf16[3,4,2,96,128]{4,3,2,1,0:T(8,128)(2,1)}, bf16[3,4,2,96,128]{4,3,2,1,0:T(8,128)(2,1)}, u32[]{:S(2)}, u32[]{:S(2)}) %collective-permute-start) | collective-permute-done | bytes 589856 | tf_op jit(solution)/shard_map/ppermute | solution.py:293
  38.1 0.0 copy-done.6
  38.1 5.3 %past_sums.1 = (f32[2,6,96,256]{3,2,1,0:T(8,128)}, f32[2,4,96,256]{3,2,1,0:T(8,128)}) custom-call(s32[2]{0:T(128)S(1)} %pad_add_fusion.place_ref, s32[64]{0:T(128)S(1)} %select_reduce_fusion.session_of_ref, s32[64]{0:T(128)S(1)} %copy-done.6, bf16[2,4,4,2,96,128]{5,4,3,2,1,0:T(8,128)(2,1)S(1)} %bitcast.29, ...), custom_call_target="tpu_custom_call" | custom-call | flops 4000000000 | bytes 6000000 | tf_op jit(solution)/shard_map/past_sums/pallas_call | solution.py:67
  43.4 5.3 %all-to-all-done.1.own_ref = bf16[16,4,24,128]{3,2,1,0:T(8,128)(2,1)S(1)} async-done(((bf16[16,4,24,128]{3,2,1,0:T(8,128)(2,1)}), bf16[16,4,24,128]{3,2,1,0:T(8,128)(2,1)S(1)}, u32[]{:S(2)}, u32[]{:S(2)}) %all-to-all-start.1) | async-done | bytes 393248 | tf_op jit(solution)/shard_map/all_to_all | solution.py:272
  48.8 1.9 %collective-permute-start.3 = (bf16[8,4,24,128]{3,2,1,0:T(8,128)(2,1)S(1)}, bf16[8,4,24,128]{3,2,1,0:T(8,128)(2,1)S(1)}, u32[]{:S(2)}, u32[]{:S(2)}) collective-permute-start(bf16[8,4,24,128]{3,2,1,0:T(8,128)(2,1)S(1)} %get-tuple-element.43), channel_id=1, source_target_pairs={{0,1},{1,2},{2,3},{3,4},{4,5},{5,6},{6,7},{7,8},{8,9},{9,10},{10,1... | collective-permute-start | bytes 589832 | tf_op jit(solution)/shard_map/ppermute | solution.py:302
  50.7 5.5 %collective-permute-start.2 = (bf16[8,4,24,128]{3,2,1,0:T(8,128)(2,1)S(1)}, bf16[8,4,24,128]{3,2,1,0:T(8,128)(2,1)S(1)}, u32[]{:S(2)}, u32[]{:S(2)}) collective-permute-start(bf16[8,4,24,128]{3,2,1,0:T(8,128)(2,1)S(1)} %get-tuple-element.44), channel_id=1, source_target_pairs={{1,0},{2,1},{3,2},{4,3},{5,4},{6,5},{7,6},{8,7},{9,8},{10,9},{11,1... | collective-permute-start | bytes 589832 | tf_op jit(solution)/shard_map/ppermute | solution.py:303
  56.2 0.0 copy-done.8
  56.2 0.1 copy.40.g_one_ref
  56.3 0.0 copy-done.9
  56.3 0.1 copy.41.g_two_ref
  56.4 2.0 %own_rows.1 = (bf16[2,1152,256]{2,1,0:T(8,128)(2,1)S(1)}, bf16[2,576,256]{2,1,0:T(8,128)(2,1)S(1)}, f32[2,6,96,256]{3,2,1,0:T(8,128)S(1)}, f32[2,4,96,256]{3,2,1...) custom-call(bf16[16,4,24,128]{3,2,1,0:T(8,128)(2,1)S(1)} %all-to-all-done.1.own_ref, ...), custom_call_target="tpu_custom_call" | custom-call | flops 1000000000 | bytes 4000000 | tf_op jit(solution)/shard_map/own_rows/pallas_call | solution.py:135
  58.4 0.6 collective-permute-done.3.halo_ref
  59.1 0.0 copy-done.2
  59.1 1.7 %top_rows.1.rest_0_ = bf16[16,4,24,128]{3,2,1,0:T(8,128)(2,1)S(1)} custom-call(s32[2]{0:T(128)S(1)} %pad_add_fusion.place_ref, s32[64]{0:T(128)S(1)} %select_reduce_fusion.session_of_ref, s32[64]{0:T(128)S(1)} %copy-done.2, bf16[8,4,24,128]{3,2,1,0:T(8,128)(2,1)S(1)} %collective-permute-done.3.halo_ref, bf16[16,4,24,128]{3,2,1,0:T(8,128)(2,1)S(1)} %all-to-all-done.1.own_ref, ...), custom_call_target="tpu_custom_call" | custom-call | flops 1000000000 | bytes 4000000 | tf_op jit(solution)/shard_map/top_rows/pallas_call | solution.py:206
  60.8 0.0 collective-permute-done.2.halo_ref
  60.9 1.6 %bottom_rows.1 = bf16[16,4,24,128]{3,2,1,0:T(8,128)(2,1)S(1)} custom-call(s32[2]{0:T(128)S(1)} %pad_add_fusion.place_ref, s32[64]{0:T(128)S(1)} %select_reduce_fusion.session_of_ref, s32[64]{0:T(128)S(1)} %copy-done.2, bf16[8,4,24,128]{3,2,1,0:T(8,128)(2,1)S(1)} %collective-permute-done.2.halo_ref, ...), custom_call_target="tpu_custom_call", output_to_operand_aliasing={{}: (13, {})} | custom-call | flops 1000000000 | bytes 4000000 | tf_op jit(solution)/shard_map/bottom_rows/pallas_call | solution.py:206
  62.5 17.8 %all_to_all.20 = bf16[16,4,24,128]{3,2,1,0:T(8,128)(2,1)S(1)} all-to-all(bf16[16,4,24,128]{3,2,1,0:T(8,128)(2,1)S(1)} %bottom_rows.1), channel_id=1, replica_groups=mesh['sess'=16,'band'=32] {'sess'}, dimensions={0} | all-to-all | bytes 786432 | tf_op jit(solution)/shard_map/all_to_all | solution.py:272
  80.2 0.6 take_in_vmem.1
  80.9 17.2 %all_to_all.21 = bf16[16,4,24,128]{3,2,1,0:T(8,128)(2,1)S(1)} all-to-all(bf16[16,4,24,128]{3,2,1,0:T(8,128)(2,1)S(1)} %bitcast.31), channel_id=1, replica_groups=mesh['sess'=16,'band'=32] {'sess'}, dimensions={0} | all-to-all | bytes 786432 | tf_op jit(solution)/shard_map/all_to_all | solution.py:272
  98.1 1.1 %copy.46 = bf16[4,4,4,24,128]{4,0,3,1,2:T(4,128)(2,1)} copy(bf16[4,4,4,24,128]{4,3,2,1,0:T(8,128)(2,1)S(1)} %bitcast.32) | data formatting | bytes 786432 | tf_op jit(solution)/shard_map/reshape | solution.py:312
  (7 shorter events, 0.1 us)
Async XLA Ops:
  0.0 9.8 %copy-start.7 = (bf16[4,2,2,96,4,128]{5,4,3,2,1,0:T(4,128)(2,1)S(1)}, bf16[4,2,2,96,4,128]{5,4,3,2,1,0:T(4,128)(2,1)}, u32[]{:S(2)}) copy-start(bf16[4,2,2,96,4,128]{5,4,3,2,1,0:T(4,128)(2,1)} %param.10) | copy-start | bytes 4718596
  2.0 23.3 %all-to-all-start = ((bf16[16,4,24,128]{3,2,1,0:T(8,128)(2,1)}), bf16[16,4,24,128]{3,2,1,0:T(8,128)(2,1)S(1)}, u32[]{:S(2)}, u32[]{:S(2)}) async-start(bf16[16,4,24,128]{3,2,1,0:T(8,128)(2,1)} %bitcast.4), calls=%async_computation | async-start | bytes 786432 | tf_op jit(solution)/shard_map/all_to_all | solution.py:272
  10.2 14.9 %copy-start.3 = (s32[64]{0:T(128)S(1)}, s32[64]{0:T(128)}, u32[]{:S(2)}) copy-start(s32[64]{0:T(128)} %slots_ref.1) | copy-start | bytes 772
  11.1 23.0 %copy-start = (bf16[96,2592]{1,0:T(8,128)(2,1)S(1)}, bf16[96,2592]{1,0:T(8,128)(2,1)}, u32[]{:S(2)}) copy-start(bf16[96,2592]{1,0:T(8,128)(2,1)} %one_ref.1) | copy-start | bytes 1492996
  11.1 23.0 %copy-start.1 = (bf16[96,2592]{1,0:T(8,128)(2,1)S(1)}, bf16[96,2592]{1,0:T(8,128)(2,1)}, u32[]{:S(2)}) copy-start(bf16[96,2592]{1,0:T(8,128)(2,1)} %two_ref.1) | copy-start | bytes 1492996
  11.1 25.0 %collective-permute-start.1 = (bf16[3,4,2,96,128]{4,3,2,1,0:T(8,128)(2,1)}, bf16[3,4,2,96,128]{4,3,2,1,0:T(8,128)(2,1)}, u32[]{:S(2)}, u32[]{:S(2)}) collective-permute-start(bf16[3,4,2,96,128]{4,3,2,1,0:T(8,128)(2,1)} %pad_maximum_fusion.1), channel_id=1, source_target_pairs={{0,1},{1,2},{2,3},{3,4},{4,5},{5,6},{6,7},{7,8},{8,9},{9,10},{10,1... | collective-permute-start | bytes 1769480 | tf_op jit(solution)/shard_map/ppermute | solution.py:294
  16.2 22.0 %copy-start.6 = (s32[64]{0:T(128)S(1)}, s32[64]{0:T(128)}, u32[]{:S(2)}) copy-start(s32[64]{0:T(128)} %counts_ref.1) | copy-start | bytes 772
  16.2 21.9 %collective-permute-start = (bf16[3,4,2,96,128]{4,3,2,1,0:T(8,128)(2,1)}, bf16[3,4,2,96,128]{4,3,2,1,0:T(8,128)(2,1)}, u32[]{:S(2)}, u32[]{:S(2)}) collective-permute-start(bf16[3,4,2,96,128]{4,3,2,1,0:T(8,128)(2,1)} %pad_maximum_fusion), channel_id=1, source_target_pairs={{1,0},{2,1},{3,2},{4,3},{5,4},{6,5},{7,6},{8,7},{9,8},{10,9},{11,1... | collective-permute-start | bytes 1769480 | tf_op jit(solution)/shard_map/ppermute | solution.py:293
  26.7 22.0 %all-to-all-start.1 = ((bf16[16,4,24,128]{3,2,1,0:T(8,128)(2,1)}), bf16[16,4,24,128]{3,2,1,0:T(8,128)(2,1)S(1)}, u32[]{:S(2)}, u32[]{:S(2)}) async-start(bf16[16,4,24,128]{3,2,1,0:T(8,128)(2,1)} %bitcast.6), calls=%async_computation.1 | async-start | bytes 786432 | tf_op jit(solution)/shard_map/all_to_all | solution.py:272
  34.5 0.7 copy-start.4
  35.1 0.7 copy-start.5
  38.1 18.0 %copy-start.8 = (f32[96]{0:T(128)S(1)}, f32[96]{0:T(128)}, u32[]{:S(2)}) copy-start(f32[96]{0:T(128)} %param.16) | copy-start | bytes 1156
  38.1 18.2 %copy-start.9 = (f32[96]{0:T(128)S(1)}, f32[96]{0:T(128)}, u32[]{:S(2)}) copy-start(f32[96]{0:T(128)} %param.17) | copy-start | bytes 1156
  48.8 10.3 %collective-permute-start.3 = (bf16[8,4,24,128]{3,2,1,0:T(8,128)(2,1)S(1)}, bf16[8,4,24,128]{3,2,1,0:T(8,128)(2,1)S(1)}, u32[]{:S(2)}, u32[]{:S(2)}) collective-permute-start(bf16[8,4,24,128]{3,2,1,0:T(8,128)(2,1)S(1)} %get-tuple-element.43), channel_id=1, source_target_pairs={{0,1},{1,2},{2,3},{3,4},{4,5},{5,6},{6,7},{7,8},{8,9},{9,10},{10,1... | collective-permute-start | bytes 589832 | tf_op jit(solution)/shard_map/ppermute | solution.py:302
  50.7 10.2 %collective-permute-start.2 = (bf16[8,4,24,128]{3,2,1,0:T(8,128)(2,1)S(1)}, bf16[8,4,24,128]{3,2,1,0:T(8,128)(2,1)S(1)}, u32[]{:S(2)}, u32[]{:S(2)}) collective-permute-start(bf16[8,4,24,128]{3,2,1,0:T(8,128)(2,1)S(1)} %get-tuple-element.44), channel_id=1, source_target_pairs={{1,0},{2,1},{3,2},{4,3},{5,4},{6,5},{7,6},{8,7},{9,8},{10,9},{11,1... | collective-permute-start | bytes 589832 | tf_op jit(solution)/shard_map/ppermute | solution.py:303
  56.4 2.7 %copy-start.2 = (s32[64]{0:T(128)S(1)}, s32[64]{0:T(128)}, u32[]{:S(2)}) copy-start(s32[64]{0:T(128)} %active_ref.3) | copy-start | bytes 772

commit v4 on v3

--- a/solution.py
+++ b/solution.py
@@ -152,7 +152,7 @@
 
 
 def side_kernel(place_ref, session_of_ref, active_ref, halo_ref, own_ref, own_cols_ref, mid_acts_ref, one_ref, two_ref, w_one_ref, w_two_ref, g_one_ref, g_two_ref, *rest, top, bands):
-    out_ref, cols_ref, acts_ref = rest[-3:]
+    out_ref, cols_ref, edge_ref = rest[-3:]
     channels = w_one_ref.shape[0]
     sessions, part = own_ref.shape[1], own_ref.shape[2]
     width = own_ref.shape[3]
@@ -161,31 +161,38 @@
     step = 3 * channels
     inside = ((place_ref[1] > 0) if top else (place_ref[1] < bands - 1)).astype(F32)
     g_one, g_two = g_one_ref[...], g_two_ref[...]
-    halo_at, own_at = (0, 2) if top else (2, 0)
+
+
+    def split_dot(w_ref, row, side, inner):
+        count = 2 - row if top else 1 + row
+        if top:
+            near = side[(2 - count) * step : 2 * step, :]
+            far = inner[: (3 - count) * step, :]
+            near_w, far_w = w_ref[:, : count * step], w_ref[:, count * step :]
+        else:
+            near = side[: count * step, :]
+            far = inner[(count - 1) * step : 2 * step, :]
+            near_w, far_w = w_ref[:, (3 - count) * step :], w_ref[:, : (3 - count) * step]
+        return jnp.dot(near_w, near, preferred_element_type=F32) + jnp.dot(far_w, far, preferred_element_type=F32)
+
     for pair in range(sessions // 2):
         for row in range(2):
             for half in range(2):
                 act = norm_silu(frame_row(halo_ref, row, 2 * pair + half, parts), g_one)
-                store_taps(cols_ref.at[pair], (halo_at + row) * step, channels, half, act)
-        from_row = 0 if top else rows - 2
-        cols_ref[pair, own_at * step : (own_at + 2) * step, :] = own_cols_ref[pair, from_row * step : (from_row + 2) * step, :]
-        acts_ref[pair, own_at * step : (own_at + 2) * step, :] = mid_acts_ref[pair]
+                store_taps(cols_ref.at[pair], row * step, channels, half, act)
     first = 0 if top else rows
+    from_row = 0 if top else rows - 2
     for pair in range(sessions // 2):
         for row in range(2):
-            hidden = one_ref[pair, first + row] + jnp.dot(
-                w_one_ref[...], cols_ref[pair, row * step : (row + 3) * step, :], preferred_element_type=F32
-            )
+            hidden = one_ref[pair, first + row] + split_dot(w_one_ref, row, cols_ref.at[pair], own_cols_ref.at[pair, pl.ds(from_row * step, 2 * step)])
             act = norm_silu(hidden, g_two)
             if row == (0 if top else 1):
                 act = act * inside
-            store_act(acts_ref, pair, halo_at + row, act)
+            store_act(edge_ref, pair, row, act)
     first = 0 if top else rows - 2
     for pair in range(sessions // 2):
         for row in range(2):
-            hidden = two_ref[pair, first + row] + jnp.dot(
-                w_two_ref[...], acts_ref[pair, row * step : (row + 3) * step, :], preferred_element_type=F32
-            )
+            hidden = two_ref[pair, first + row] + split_dot(w_two_ref, row, edge_ref.at[pair], mid_acts_ref.at[pair])
             for half in range(2):
                 session = 2 * pair + half
                 active = active_ref[session_of_ref[place_ref[0] * sessions + session]].astype(F32)
@@ -209,7 +216,7 @@
         out_specs=vmem,
         out_shape=jax.ShapeDtypeStruct(own.shape, BF16),
         input_output_aliases={} if earlier is None else {len(operands) - 1: 0},
-        scratch_shapes=[pltpu.VMEM((pairs, 4 * step, lanes), BF16), pltpu.VMEM((pairs, 4 * step, lanes), BF16)],
+        scratch_shapes=[pltpu.VMEM((pairs, 2 * step, lanes), BF16), pltpu.VMEM((pairs, 2 * step, lanes), BF16)],
         compiler_params=pltpu.CompilerParams(vmem_limit_bytes=16 * 1024 * 1024),
         cost_estimate=pl.CostEstimate(flops=10**9, bytes_accessed=4 * 10**6, transcendentals=10**6),
         name="top_rows" if top else "bottom_rows",
@@ -240,15 +247,29 @@
     )(one, two)
 
 
-def take_slots(pieces, slots):
-    return lax.gather(
-        pieces,
-        slots[:, None],
-        lax.GatherDimensionNumbers(offset_dims=(1, 2), collapsed_slice_dims=(0,), start_index_map=(0,)),
-        slice_sizes=(1,) + pieces.shape[1:],
-        unique_indices=True,
-        mode=lax.GatherScatterMode.CLIP,
-    )
+def send_kernel(slots_ref, in_ref, out_hbm, buf_ref, sems):
+    chunk = in_ref.shape[0] // sems.shape[0]
+    copies = []
+    for i in range(sems.shape[0]):
+        for slot in range(i * chunk, (i + 1) * chunk):
+            buf_ref[slot] = in_ref[slots_ref[slot]]
+        block = pl.ds(i * chunk, chunk)
+        copies.append(pltpu.make_async_copy(buf_ref.at[block], out_hbm.at[block], sems.at[i]))
+        copies[-1].start()
+    for copy in copies:
+        copy.wait()
+
+
+def take_to_hbm(pieces, slots):
+    return pl.pallas_call(
+        send_kernel,
+        in_specs=[pl.BlockSpec(memory_space=pltpu.SMEM), pl.BlockSpec(memory_space=pltpu.VMEM)],
+        out_specs=pl.BlockSpec(memory_space=pltpu.HBM),
+        out_shape=pltpu.HBM(pieces.shape, pieces.dtype),
+        scratch_shapes=[pltpu.VMEM(pieces.shape, pieces.dtype), pltpu.SemaphoreType.DMA((4,))],
+        compiler_params=pltpu.CompilerParams(vmem_limit_bytes=4 * 1024 * 1024),
+        name="take_to_hbm",
+    )(slots, pieces)
 
 
 def take_kernel(slots_ref, in_ref, out_ref):
@@ -295,7 +316,7 @@
     past_one, past_two, new_one, new_two = split_weights(weight_one, weight_two)
     one, two = past_sums(place, session_of, counts, own, above, below, past_one, past_two)
 
-    sorted_pieces = take_slots(spread.reshape(-1, part, width), session_of)
+    sorted_pieces = take_to_hbm(spread.reshape(-1, part, width), session_of)
     held = exchange(sorted_pieces.reshape(sess_count, sessions, part, width))
     held, one, two = lax.optimization_barrier((held, one, two))
     half = sess_count - 2 * parts

time: 99.6 us -> 99.5 us (level)
  local copies, waits for them, and re-layouts: 6.44 us -> 5 us
  Pallas kernels: 11.5 us -> 12.9 us
    gather x1 -> x0, local copies, waits for them, and re-layouts: 1.38 us -> none  [take_slots(): lax.gather(pieces, slots[:, None], lax.GatherDimensionNumbers(offset_dims...]
    pallas_call x0 -> x1, Pallas kernels: none -> 1.33 us  [take_to_hbm(): pl.pallas_call(send_kernel, in_specs=[pl.BlockSpec(memory_space=pltpu.SME...]
    unnamed x21 -> x20, local copies, waits for them, and re-layouts: 2.53 us -> 1.36 us
    optimization_barrier x2, local copies, waits for them, and re-layouts: 1.14 us -> 2.26 us  [local(): cut, cache = lax.optimization_barrier((cut, cache))]
  transfers between devices with their start and end apart: 6 -> 6, of which waited for: 4 -> 5; matrix products, arithmetic and copies ran while one was open for 4% -> 3% of each run, Pallas kernels for 9% -> 11%
where the time goes in v4:
time: 99.5 us; the launch traced here: 99 us
  starting transfers between devices  35.8 us (36%)
  blocking collectives  34.9 us (35%)
  Pallas kernels  12.9 us (13%)
  waiting for transfers between devices  8.2 us (8%)
  local copies, waits for them, and re-layouts  5 us (5%)
  other arithmetic  1.95 us (2%)
    all_to_all x2, blocking collectives, exchange(): return lax.all_to_all(pieces, 'sess', 0, 0, tiled=True)  34.9 us
    all_to_all x2, starting transfers between devices, exchange(): return lax.all_to_all(pieces, 'sess', 0, 0, tiled=True)  15.3 us
    ppermute x1, starting transfers between devices, local(): below = lax.ppermute(jnp.concatenate([own[0, :2], own[1, :1]]), 'band', up)  8.97 us
    ppermute x1, starting transfers between devices, local(): held_below = lax.ppermute(held[:2 * parts], 'band', up)  5.47 us
    pallas_call x1, Pallas kernels, past_sums(): pl.pallas_call(past_kernel, in_specs=[smem, smem, smem, vmem, vmem, vmem,...  5.35 us
    all_to_all x2, waiting for transfers between devices, exchange(): return lax.all_to_all(pieces, 'sess', 0, 0, tiled=True)  5.19 us
    ppermute x1, starting transfers between devices, local(): lax.ppermute(jnp.concatenate([own[0, rows - 2:], own[1, rows - 1:]]), 'ba...  4.14 us
    pallas_call x2, Pallas kernels, side_rows(): pl.pallas_call(functools.partial(side_kernel, top=top, bands=bands), in_s...  3.32 us
  transfers between devices with their start and end apart: 6, of which 5 were waited for; matrix products, arithmetic and copies ran while one was open for 3% of the time, Pallas kernels for 11%

profile of v4, /device:TPU:7, one launch (start us, length us, event | category | flops | bytes accessed | tf_op | source)
XLA Modules:
  0.0 99.0 jit_solution(16468759293668268234)
XLA Ops:
  0.0 0.0 copy-start.7
  0.0 1.9 %copy.20 = bf16[4,4,4,24,128]{4,3,2,1,0:T(8,128)(2,1)} copy(bf16[4,4,4,24,128]{4,0,3,1,2:T(4,128)(2,1)} %bitcast.35) | data formatting | bytes 786432 | tf_op jit(solution)/shard_map/optimization_barrier | solution.py:310
  1.9 7.8 %all-to-all-start = ((bf16[16,4,24,128]{3,2,1,0:T(8,128)(2,1)}), bf16[16,4,24,128]{3,2,1,0:T(8,128)(2,1)S(1)}, u32[]{:S(2)}, u32[]{:S(2)}) async-start(bf16[16,4,24,128]{3,2,1,0:T(8,128)(2,1)} %bitcast.4), calls=%async_computation | async-start | bytes 786432 | tf_op jit(solution)/shard_map/all_to_all | solution.py:293
  9.7 0.0 copy-done.7
  9.7 0.4 copy.30
  10.1 0.1 slice_bitcast_fusion
  10.2 0.0 copy-start.3
  10.2 0.9 pad_maximum_fusion.1
  11.1 0.0 copy-start
  11.1 4.1 %collective-permute-start.1 = (bf16[3,4,2,96,128]{4,3,2,1,0:T(8,128)(2,1)}, bf16[3,4,2,96,128]{4,3,2,1,0:T(8,128)(2,1)}, u32[]{:S(2)}, u32[]{:S(2)}) collective-permute-start(bf16[3,4,2,96,128]{4,3,2,1,0:T(8,128)(2,1)} %pad_maximum_fusion.1), channel_id=1, source_target_pairs={{0,1},{1,2},{2,3},{3,4},{4,5},{5,6},{6,7},{7,8},{8,9},{9,10},{10,1... | collective-permute-start | bytes 1769480 | tf_op jit(solution)/shard_map/ppermute | solution.py:315
  15.2 0.9 pad_maximum_fusion
  16.1 0.0 copy-start.6
  16.1 9.0 %collective-permute-start = (bf16[3,4,2,96,128]{4,3,2,1,0:T(8,128)(2,1)}, bf16[3,4,2,96,128]{4,3,2,1,0:T(8,128)(2,1)}, u32[]{:S(2)}, u32[]{:S(2)}) collective-permute-start(bf16[3,4,2,96,128]{4,3,2,1,0:T(8,128)(2,1)} %pad_maximum_fusion), channel_id=1, source_target_pairs={{1,0},{2,1},{3,2},{4,3},{5,4},{6,5},{7,6},{8,7},{9,8},{10,9},{11,1... | collective-permute-start | bytes 1769480 | tf_op jit(solution)/shard_map/ppermute | solution.py:314
  25.1 0.0 copy-done.3
  25.1 0.1 select_reduce_fusion.slots_ref.session_of_ref
  25.2 0.0 all-to-all-done
  25.2 1.3 %take_to_hbm.1 = bf16[64,24,128]{2,1,0:T(8,128)(2,1)} custom-call(s32[64]{0:T(128)S(1)} %select_reduce_fusion.slots_ref.session_of_ref, bf16[64,24,128]{2,1,0:T(8,128)(2,1)S(1)} %bitcast.30), custom_call_target="tpu_custom_call" | custom-call | tf_op jit(solution)/shard_map/take_to_hbm/pallas_call | solution.py:264
  26.6 7.5 %all-to-all-start.1 = ((bf16[16,4,24,128]{3,2,1,0:T(8,128)(2,1)}), bf16[16,4,24,128]{3,2,1,0:T(8,128)(2,1)S(1)}, u32[]{:S(2)}, u32[]{:S(2)}) async-start(bf16[16,4,24,128]{3,2,1,0:T(8,128)(2,1)} %bitcast.34), calls=%async_computation.1 | async-start | bytes 786432 | tf_op jit(solution)/shard_map/all_to_all | solution.py:293
  34.0 0.0 copy-done
  34.1 0.0 copy-done.1
  34.1 0.3 split_weights.1
  34.4 0.0 copy-start.4
  34.4 0.6 copy-done.4
  35.0 0.0 copy-start.5
  35.0 0.7 copy-done.5
  35.7 0.1 pad_add_fusion.place_ref
  35.8 0.3 collective-permute-done.1.above_ref
  36.0 2.0 %collective-permute-done.below_ref = bf16[3,4,2,96,128]{4,3,2,1,0:T(8,128)(2,1)} collective-permute-done((bf16[3,4,2,96,128]{4,3,2,1,0:T(8,128)(2,1)}, bf16[3,4,2,96,128]{4,3,2,1,0:T(8,128)(2,1)}, u32[]{:S(2)}, u32[]{:S(2)}) %collective-permute-start) | collective-permute-done | bytes 589856 | tf_op jit(solution)/shard_map/ppermute | solution.py:314
  38.0 0.0 copy-done.6
  38.1 0.0 copy-start.8
  38.1 5.3 %past_sums.1 = (f32[2,6,96,256]{3,2,1,0:T(8,128)}, f32[2,4,96,256]{3,2,1,0:T(8,128)}) custom-call(s32[2]{0:T(128)S(1)} %pad_add_fusion.place_ref, s32[64]{0:T(128)S(1)} %select_reduce_fusion.slots_ref.session_of_ref, s32[64]{0:T(128)S(1)} %copy-done.6, bf16[2,4,4,2,96,128]{5,4,3,2,1,0:T(8,128)(2,1)S(1)} %bitcast.29, ...), custom_call_target="tpu_custom_call" | custom-call | flops 4000000000 | bytes 6000000 | tf_op jit(solution)/shard_map/past_sums/pallas_call | solution.py:67
  43.4 5.2 %all-to-all-done.1.own_ref = bf16[16,4,24,128]{3,2,1,0:T(8,128)(2,1)S(1)} async-done(((bf16[16,4,24,128]{3,2,1,0:T(8,128)(2,1)}), bf16[16,4,24,128]{3,2,1,0:T(8,128)(2,1)S(1)}, u32[]{:S(2)}, u32[]{:S(2)}) %all-to-all-start.1) | async-done | bytes 393248 | tf_op jit(solution)/shard_map/all_to_all | solution.py:293
  48.6 1.9 %collective-permute-start.3 = (bf16[8,4,24,128]{3,2,1,0:T(8,128)(2,1)S(1)}, bf16[8,4,24,128]{3,2,1,0:T(8,128)(2,1)S(1)}, u32[]{:S(2)}, u32[]{:S(2)}) collective-permute-start(bf16[8,4,24,128]{3,2,1,0:T(8,128)(2,1)S(1)} %get-tuple-element.43), channel_id=1, source_target_pairs={{0,1},{1,2},{2,3},{3,4},{4,5},{5,6},{6,7},{7,8},{8,9},{9,10},{10,1... | collective-permute-start | bytes 589832 | tf_op jit(solution)/shard_map/ppermute | solution.py:323
  50.6 5.5 %collective-permute-start.2 = (bf16[8,4,24,128]{3,2,1,0:T(8,128)(2,1)S(1)}, bf16[8,4,24,128]{3,2,1,0:T(8,128)(2,1)S(1)}, u32[]{:S(2)}, u32[]{:S(2)}) collective-permute-start(bf16[8,4,24,128]{3,2,1,0:T(8,128)(2,1)S(1)} %get-tuple-element.44), channel_id=1, source_target_pairs={{1,0},{2,1},{3,2},{4,3},{5,4},{6,5},{7,6},{8,7},{9,8},{10,9},{11,1... | collective-permute-start | bytes 589832 | tf_op jit(solution)/shard_map/ppermute | solution.py:324
  56.1 0.0 copy-done.8
  56.1 0.1 copy.22.g_one_ref
  56.2 0.0 copy-done.9
  56.2 0.1 copy.23.g_two_ref
  56.3 2.0 %own_rows.1 = (bf16[2,1152,256]{2,1,0:T(8,128)(2,1)S(1)}, bf16[2,576,256]{2,1,0:T(8,128)(2,1)S(1)}, f32[2,6,96,256]{3,2,1,0:T(8,128)S(1)}, f32[2,4,96,256]{3,2,1...) custom-call(bf16[16,4,24,128]{3,2,1,0:T(8,128)(2,1)S(1)} %all-to-all-done.1.own_ref, ...), custom_call_target="tpu_custom_call" | custom-call | flops 1000000000 | bytes 4000000 | tf_op jit(solution)/shard_map/own_rows/pallas_call | solution.py:135
  58.3 0.6 collective-permute-done.3.halo_ref
  59.0 0.0 copy-done.2
  59.0 1.7 %top_rows.1.rest_0_ = bf16[16,4,24,128]{3,2,1,0:T(8,128)(2,1)S(1)} custom-call(s32[2]{0:T(128)S(1)} %pad_add_fusion.place_ref, s32[64]{0:T(128)S(1)} %select_reduce_fusion.slots_ref.session_of_ref, s32[64]{0:T(128)S(1)} %copy-done.2, bf16[8,4,24,128]{3,2,1,0:T(8,128)(2,1)S(1)} %collective-permute-done.3.halo_ref, ...), custom_call_target="tpu_custom_call" | custom-call | flops 1000000000 | bytes 4000000 | tf_op jit(solution)/shard_map/top_rows/pallas_call | solution.py:213
  60.7 0.1 collective-permute-done.2.halo_ref
  60.7 1.6 %bottom_rows.1 = bf16[16,4,24,128]{3,2,1,0:T(8,128)(2,1)S(1)} custom-call(s32[2]{0:T(128)S(1)} %pad_add_fusion.place_ref, s32[64]{0:T(128)S(1)} %select_reduce_fusion.slots_ref.session_of_ref, s32[64]{0:T(128)S(1)} %copy-done.2, bf16[8,4,24,128]{3,2,1,0:T(8,128)(2,1)S(1)} %collective-permute-done.2.halo_ref, ...), custom_call_target="tpu_custom_call", output_to_operand_aliasing={{}: (13, {})} | custom-call | flops 1000000000 | bytes 4000000 | tf_op jit(solution)/shard_map/bottom_rows/pallas_call | solution.py:213
  62.4 17.7 %all_to_all.20 = bf16[16,4,24,128]{3,2,1,0:T(8,128)(2,1)S(1)} all-to-all(bf16[16,4,24,128]{3,2,1,0:T(8,128)(2,1)S(1)} %bottom_rows.1), channel_id=1, replica_groups=mesh['sess'=16,'band'=32] {'sess'}, dimensions={0} | all-to-all | bytes 786432 | tf_op jit(solution)/shard_map/all_to_all | solution.py:293
  80.1 0.6 take_in_vmem.1
  80.7 17.2 %all_to_all.21 = bf16[16,4,24,128]{3,2,1,0:T(8,128)(2,1)S(1)} all-to-all(bf16[16,4,24,128]{3,2,1,0:T(8,128)(2,1)S(1)} %bitcast.32), channel_id=1, replica_groups=mesh['sess'=16,'band'=32] {'sess'}, dimensions={0} | all-to-all | bytes 786432 | tf_op jit(solution)/shard_map/all_to_all | solution.py:293
  97.9 1.1 %copy.28 = bf16[4,4,4,24,128]{4,0,3,1,2:T(4,128)(2,1)} copy(bf16[4,4,4,24,128]{4,3,2,1,0:T(8,128)(2,1)S(1)} %bitcast.33) | data formatting | bytes 786432 | tf_op jit(solution)/shard_map/reshape | solution.py:333
  (5 shorter events, 0.1 us)
Async XLA Ops:
  0.0 9.7 %copy-start.7 = (bf16[4,2,2,96,4,128]{5,4,3,2,1,0:T(4,128)(2,1)S(1)}, bf16[4,2,2,96,4,128]{5,4,3,2,1,0:T(4,128)(2,1)}, u32[]{:S(2)}) copy-start(bf16[4,2,2,96,4,128]{5,4,3,2,1,0:T(4,128)(2,1)} %param.10) | copy-start | bytes 4718596
  1.9 23.3 %all-to-all-start = ((bf16[16,4,24,128]{3,2,1,0:T(8,128)(2,1)}), bf16[16,4,24,128]{3,2,1,0:T(8,128)(2,1)S(1)}, u32[]{:S(2)}, u32[]{:S(2)}) async-start(bf16[16,4,24,128]{3,2,1,0:T(8,128)(2,1)} %bitcast.4), calls=%async_computation | async-start | bytes 786432 | tf_op jit(solution)/shard_map/all_to_all | solution.py:293
  10.2 14.9 %copy-start.3 = (s32[64]{0:T(128)S(1)}, s32[64]{0:T(128)}, u32[]{:S(2)}) copy-start(s32[64]{0:T(128)} %slots_ref.1) | copy-start | bytes 772
  11.1 23.0 %copy-start = (bf16[96,2592]{1,0:T(8,128)(2,1)S(1)}, bf16[96,2592]{1,0:T(8,128)(2,1)}, u32[]{:S(2)}) copy-start(bf16[96,2592]{1,0:T(8,128)(2,1)} %one_ref.1) | copy-start | bytes 1492996
  11.1 23.0 %copy-start.1 = (bf16[96,2592]{1,0:T(8,128)(2,1)S(1)}, bf16[96,2592]{1,0:T(8,128)(2,1)}, u32[]{:S(2)}) copy-start(bf16[96,2592]{1,0:T(8,128)(2,1)} %two_ref.1) | copy-start | bytes 1492996
  11.1 25.0 %collective-permute-start.1 = (bf16[3,4,2,96,128]{4,3,2,1,0:T(8,128)(2,1)}, bf16[3,4,2,96,128]{4,3,2,1,0:T(8,128)(2,1)}, u32[]{:S(2)}, u32[]{:S(2)}) collective-permute-start(bf16[3,4,2,96,128]{4,3,2,1,0:T(8,128)(2,1)} %pad_maximum_fusion.1), channel_id=1, source_target_pairs={{0,1},{1,2},{2,3},{3,4},{4,5},{5,6},{6,7},{7,8},{8,9},{9,10},{10,1... | collective-permute-start | bytes 1769480 | tf_op jit(solution)/shard_map/ppermute | solution.py:315
  16.1 22.0 %copy-start.6 = (s32[64]{0:T(128)S(1)}, s32[64]{0:T(128)}, u32[]{:S(2)}) copy-start(s32[64]{0:T(128)} %counts_ref.1) | copy-start | bytes 772
  16.1 21.9 %collective-permute-start = (bf16[3,4,2,96,128]{4,3,2,1,0:T(8,128)(2,1)}, bf16[3,4,2,96,128]{4,3,2,1,0:T(8,128)(2,1)}, u32[]{:S(2)}, u32[]{:S(2)}) collective-permute-start(bf16[3,4,2,96,128]{4,3,2,1,0:T(8,128)(2,1)} %pad_maximum_fusion), channel_id=1, source_target_pairs={{1,0},{2,1},{3,2},{4,3},{5,4},{6,5},{7,6},{8,7},{9,8},{10,9},{11,1... | collective-permute-start | bytes 1769480 | tf_op jit(solution)/shard_map/ppermute | solution.py:314
  26.6 22.0 %all-to-all-start.1 = ((bf16[16,4,24,128]{3,2,1,0:T(8,128)(2,1)}), bf16[16,4,24,128]{3,2,1,0:T(8,128)(2,1)S(1)}, u32[]{:S(2)}, u32[]{:S(2)}) async-start(bf16[16,4,24,128]{3,2,1,0:T(8,128)(2,1)} %bitcast.34), calls=%async_computation.1 | async-start | bytes 786432 | tf_op jit(solution)/shard_map/all_to_all | solution.py:293
  34.4 0.7 copy-start.4
  35.0 0.7 copy-start.5
  38.1 18.0 %copy-start.8 = (f32[96]{0:T(128)S(1)}, f32[96]{0:T(128)}, u32[]{:S(2)}) copy-start(f32[96]{0:T(128)} %param.16) | copy-start | bytes 1156
  38.1 18.1 %copy-start.9 = (f32[96]{0:T(128)S(1)}, f32[96]{0:T(128)}, u32[]{:S(2)}) copy-start(f32[96]{0:T(128)} %param.17) | copy-start | bytes 1156
  48.6 10.3 %collective-permute-start.3 = (bf16[8,4,24,128]{3,2,1,0:T(8,128)(2,1)S(1)}, bf16[8,4,24,128]{3,2,1,0:T(8,128)(2,1)S(1)}, u32[]{:S(2)}, u32[]{:S(2)}) collective-permute-start(bf16[8,4,24,128]{3,2,1,0:T(8,128)(2,1)S(1)} %get-tuple-element.43), channel_id=1, source_target_pairs={{0,1},{1,2},{2,3},{3,4},{4,5},{5,6},{6,7},{7,8},{8,9},{9,10},{10,1... | collective-permute-start | bytes 589832 | tf_op jit(solution)/shard_map/ppermute | solution.py:323
  50.6 10.2 %collective-permute-start.2 = (bf16[8,4,24,128]{3,2,1,0:T(8,128)(2,1)S(1)}, bf16[8,4,24,128]{3,2,1,0:T(8,128)(2,1)S(1)}, u32[]{:S(2)}, u32[]{:S(2)}) collective-permute-start(bf16[8,4,24,128]{3,2,1,0:T(8,128)(2,1)S(1)} %get-tuple-element.44), channel_id=1, source_target_pairs={{1,0},{2,1},{3,2},{4,3},{5,4},{6,5},{7,6},{8,7},{9,8},{10,9},{11,1... | collective-permute-start | bytes 589832 | tf_op jit(solution)/shard_map/ppermute | solution.py:324
  56.3 2.7 %copy-start.2 = (s32[64]{0:T(128)S(1)}, s32[64]{0:T(128)}, u32[]{:S(2)}) copy-start(s32[64]{0:T(128)} %active_ref.3) | copy-start | bytes 772

commit v5 on v4

--- a/solution.py
+++ b/solution.py
@@ -28,7 +28,8 @@
 def norm_silu(values, gain):
     mean_square = jnp.mean(values * values, axis=0, keepdims=True)
     scaled = values * lax.rsqrt(mean_square + 1e-06) * gain
-    return 0.5 * scaled * (1.0 + jnp.tanh(0.5 * scaled))
+    half = 0.5 * scaled
+    return half + half * jnp.tanh(half)
 
 
 def past_kernel(place_ref, session_of_ref, counts_ref, own_ref, below_ref, above_ref, w_one_ref, w_two_ref, one_hbm, two_hbm, one_cols_ref, two_cols_ref, one_ref, two_ref, sems):
@@ -113,7 +114,7 @@
     for pair in range(pairs):
         for row in range(rows):
             for half in range(2):
-                act = norm_silu(frame_row(own_ref, row, 2 * pair + half, parts), g_one)
+                act = norm_silu(frame_row(own_ref, row, 2 * pair + half, parts), g_one[:, : own_ref.shape[3]])
                 store_taps(cols_ref.at[pair], row * step, channels, half, act)
     copies[0].wait()
     copies[1].wait()
@@ -178,7 +179,7 @@
     for pair in range(sessions // 2):
         for row in range(2):
             for half in range(2):
-                act = norm_silu(frame_row(halo_ref, row, 2 * pair + half, parts), g_one)
+                act = norm_silu(frame_row(halo_ref, row, 2 * pair + half, parts), g_one[:, :width])
                 store_taps(cols_ref.at[pair], row * step, channels, half, act)
     first = 0 if top else rows
     from_row = 0 if top else rows - 2
@@ -247,29 +248,15 @@
     )(one, two)
 
 
-def send_kernel(slots_ref, in_ref, out_hbm, buf_ref, sems):
-    chunk = in_ref.shape[0] // sems.shape[0]
-    copies = []
-    for i in range(sems.shape[0]):
-        for slot in range(i * chunk, (i + 1) * chunk):
-            buf_ref[slot] = in_ref[slots_ref[slot]]
-        block = pl.ds(i * chunk, chunk)
-        copies.append(pltpu.make_async_copy(buf_ref.at[block], out_hbm.at[block], sems.at[i]))
-        copies[-1].start()
-    for copy in copies:
-        copy.wait()
-
-
-def take_to_hbm(pieces, slots):
-    return pl.pallas_call(
-        send_kernel,
-        in_specs=[pl.BlockSpec(memory_space=pltpu.SMEM), pl.BlockSpec(memory_space=pltpu.VMEM)],
-        out_specs=pl.BlockSpec(memory_space=pltpu.HBM),
-        out_shape=pltpu.HBM(pieces.shape, pieces.dtype),
-        scratch_shapes=[pltpu.VMEM(pieces.shape, pieces.dtype), pltpu.SemaphoreType.DMA((4,))],
-        compiler_params=pltpu.CompilerParams(vmem_limit_bytes=4 * 1024 * 1024),
-        name="take_to_hbm",
-    )(slots, pieces)
+def take_slots(pieces, slots):
+    return lax.gather(
+        pieces,
+        slots[:, None],
+        lax.GatherDimensionNumbers(offset_dims=(1, 2), collapsed_slice_dims=(0,), start_index_map=(0,)),
+        slice_sizes=(1,) + pieces.shape[1:],
+        unique_indices=True,
+        mode=lax.GatherScatterMode.CLIP,
+    )
 
 
 def take_kernel(slots_ref, in_ref, out_ref):
@@ -316,13 +303,13 @@
     past_one, past_two, new_one, new_two = split_weights(weight_one, weight_two)
     one, two = past_sums(place, session_of, counts, own, above, below, past_one, past_two)
 
-    sorted_pieces = take_to_hbm(spread.reshape(-1, part, width), session_of)
+    sorted_pieces = take_slots(spread.reshape(-1, part, width), session_of)
     held = exchange(sorted_pieces.reshape(sess_count, sessions, part, width))
     held, one, two = lax.optimization_barrier((held, one, two))
     half = sess_count - 2 * parts
     held_above = lax.ppermute(held[half:], "band", down)
     held_below = lax.ppermute(held[: 2 * parts], "band", up)
-    gains = gain_one[:, None], gain_two[:, None]
+    gains = [jnp.broadcast_to(gain[:, None], (channels, 2 * width)) for gain in (gain_one, gain_two)]
     inner = own_rows(held, one, two, new_one, new_two, *gains)
     upper = side_rows(True, band_count, place, session_of, active, held_above, held, inner, *gains)
     result = side_rows(False, band_count, place, session_of, active, held_below, held, inner, *gains, earlier=upper)

time: 99.5 us -> 99.6 us (level)
  Pallas kernels: 12.9 us -> 11.5 us
  local copies, waits for them, and re-layouts: 5 us -> 6.38 us
    gather x0 -> x1, local copies, waits for them, and re-layouts: none -> 1.38 us  [take_slots(): lax.gather(pieces, slots[:, None], lax.GatherDimensionNumbers(offset_dims...]
    pallas_call x1 -> x0, Pallas kernels: 1.33 us -> none  [take_to_hbm(): pl.pallas_call(send_kernel, in_specs=[pl.BlockSpec(memory_space=pltpu.SME...]
    unnamed x20 -> x21, local copies, waits for them, and re-layouts: 1.36 us -> 2.53 us
    optimization_barrier x2, local copies, waits for them, and re-layouts: 2.26 us -> 1.14 us  [local(): cut, cache = lax.optimization_barrier((cut, cache))]
  transfers between devices with their start and end apart: 6 -> 6, of which waited for: 5 -> 5; matrix products, arithmetic and copies ran while one was open for 3% -> 4% of each run, Pallas kernels for 11% -> 9%
where the time goes in v5:
time: 99.6 us; the launch traced here: 99.1 us
  starting transfers between devices  35.8 us (36%)
  blocking collectives  34.9 us (35%)
  Pallas kernels  11.5 us (12%)
  waiting for transfers between devices  8.32 us (8%)
  local copies, waits for them, and re-layouts  6.38 us (6%)
  other arithmetic  1.96 us (2%)
    all_to_all x2, blocking collectives, exchange(): return lax.all_to_all(pieces, 'sess', 0, 0, tiled=True)  34.9 us
    all_to_all x2, starting transfers between devices, exchange(): return lax.all_to_all(pieces, 'sess', 0, 0, tiled=True)  15.3 us
    ppermute x1, starting transfers between devices, local(): below = lax.ppermute(jnp.concatenate([own[0, :2], own[1, :1]]), 'band', up)  8.97 us
    ppermute x1, starting transfers between devices, local(): held_below = lax.ppermute(held[:2 * parts], 'band', up)  5.47 us
    pallas_call x1, Pallas kernels, past_sums(): pl.pallas_call(past_kernel, in_specs=[smem, smem, smem, vmem, vmem, vmem,...  5.3 us
    all_to_all x2, waiting for transfers between devices, exchange(): return lax.all_to_all(pieces, 'sess', 0, 0, tiled=True)  5.28 us
    ppermute x1, starting transfers between devices, local(): lax.ppermute(jnp.concatenate([own[0, rows - 2:], own[1, rows - 1:]]), 'ba...  4.14 us
    pallas_call x2, Pallas kernels, side_rows(): pl.pallas_call(functools.partial(side_kernel, top=top, bands=bands), in_s...  3.31 us
  transfers between devices with their start and end apart: 6, of which 5 were waited for; matrix products, arithmetic and copies ran while one was open for 4% of the time, Pallas kernels for 9%

profile of v5, /device:TPU:7, one launch (start us, length us, event | category | flops | bytes accessed | tf_op | source)
XLA Modules:
  0.0 99.1 jit_solution(10163202581406273326)
XLA Ops:
  0.0 0.0 copy-start.7
  0.0 1.2 %copy.19 = bf16[4,96,4,128]{3,1,2,0:T(8,128)(2,1)S(1)} copy(bf16[4,96,4,128]{3,2,1,0:T(4,128)(2,1)} %param.9) | data formatting | bytes 786432 | tf_op args[0]
  1.2 0.8 copy.20
  2.0 7.8 %all-to-all-start = ((bf16[16,4,24,128]{3,2,1,0:T(8,128)(2,1)}), bf16[16,4,24,128]{3,2,1,0:T(8,128)(2,1)S(1)}, u32[]{:S(2)}, u32[]{:S(2)}) async-start(bf16[16,4,24,128]{3,2,1,0:T(8,128)(2,1)} %bitcast.4), calls=%async_computation | async-start | bytes 786432 | tf_op jit(solution)/shard_map/all_to_all | solution.py:280
  9.8 0.0 copy-done.7
  9.8 0.4 copy.24
  10.2 0.1 slice_bitcast_fusion
  10.2 0.0 copy-start.3
  10.2 0.9 pad_maximum_fusion.1
  11.1 0.0 copy-start
  11.1 0.0 copy-start.1
  11.1 4.1 %collective-permute-start.1 = (bf16[3,4,2,96,128]{4,3,2,1,0:T(8,128)(2,1)}, bf16[3,4,2,96,128]{4,3,2,1,0:T(8,128)(2,1)}, u32[]{:S(2)}, u32[]{:S(2)}) collective-permute-start(bf16[3,4,2,96,128]{4,3,2,1,0:T(8,128)(2,1)} %pad_maximum_fusion.1), channel_id=1, source_target_pairs={{0,1},{1,2},{2,3},{3,4},{4,5},{5,6},{6,7},{7,8},{8,9},{9,10},{10,1... | collective-permute-start | bytes 1769480 | tf_op jit(solution)/shard_map/ppermute | solution.py:302
  15.3 0.9 pad_maximum_fusion
  16.2 9.0 %collective-permute-start = (bf16[3,4,2,96,128]{4,3,2,1,0:T(8,128)(2,1)}, bf16[3,4,2,96,128]{4,3,2,1,0:T(8,128)(2,1)}, u32[]{:S(2)}, u32[]{:S(2)}) collective-permute-start(bf16[3,4,2,96,128]{4,3,2,1,0:T(8,128)(2,1)} %pad_maximum_fusion), channel_id=1, source_target_pairs={{1,0},{2,1},{3,2},{4,3},{5,4},{6,5},{7,6},{8,7},{9,8},{10,9},{11,1... | collective-permute-start | bytes 1769480 | tf_op jit(solution)/shard_map/ppermute | solution.py:301
  25.2 0.0 copy-done.3
  25.2 0.1 select_reduce_fusion.session_of_ref
  25.3 0.0 all-to-all-done
  25.3 1.4 %gather_fusion = bf16[64,24,128]{2,1,0:T(8,128)(2,1)} fusion(bf16[64,24,128]{2,1,0:T(8,128)(2,1)S(1)} %bitcast.32, s32[1024]{0:T(1024)S(1)} %pad_clamp_fusion), kind=kCustom, calls=%fused_computation | custom fusion | bytes 786688 | tf_op jit(solution)/shard_map/gather | solution.py:252
  26.7 7.5 %all-to-all-start.1 = ((bf16[16,4,24,128]{3,2,1,0:T(8,128)(2,1)}), bf16[16,4,24,128]{3,2,1,0:T(8,128)(2,1)S(1)}, u32[]{:S(2)}, u32[]{:S(2)}) async-start(bf16[16,4,24,128]{3,2,1,0:T(8,128)(2,1)} %bitcast.6), calls=%async_computation.1 | async-start | bytes 786432 | tf_op jit(solution)/shard_map/all_to_all | solution.py:280
  34.2 0.0 copy-done
  34.2 0.0 copy-done.1
  34.2 0.3 split_weights.1
  34.5 0.0 copy-start.4
  34.5 0.6 copy-done.4
  35.1 0.7 copy-done.5
  35.8 0.1 pad_add_fusion.place_ref
  35.9 0.2 collective-permute-done.1.above_ref
  36.1 2.0 %collective-permute-done.below_ref = bf16[3,4,2,96,128]{4,3,2,1,0:T(8,128)(2,1)} collective-permute-done((bf16[3,4,2,96,128]{4,3,2,1,0:T(8,128)(2,1)}, bf16[3,4,2,96,128]{4,3,2,1,0:T(8,128)(2,1)}, u32[]{:S(2)}, u32[]{:S(2)}) %collective-permute-start) | collective-permute-done | bytes 589856 | tf_op jit(solution)/shard_map/ppermute | solution.py:301
  38.1 0.0 copy-done.6
  38.1 5.3 %past_sums.1 = (f32[2,6,96,256]{3,2,1,0:T(8,128)}, f32[2,4,96,256]{3,2,1,0:T(8,128)}) custom-call(s32[2]{0:T(128)S(1)} %pad_add_fusion.place_ref, s32[64]{0:T(128)S(1)} %select_reduce_fusion.session_of_ref, s32[64]{0:T(128)S(1)} %copy-done.6, bf16[2,4,4,2,96,128]{5,4,3,2,1,0:T(8,128)(2,1)S(1)} %bitcast.27, ...), custom_call_target="tpu_custom_call" | custom-call | flops 4000000000 | bytes 6000000 | tf_op jit(solution)/shard_map/past_sums/pallas_call | solution.py:68
  43.4 5.3 %all-to-all-done.1.own_ref = bf16[16,4,24,128]{3,2,1,0:T(8,128)(2,1)S(1)} async-done(((bf16[16,4,24,128]{3,2,1,0:T(8,128)(2,1)}), bf16[16,4,24,128]{3,2,1,0:T(8,128)(2,1)S(1)}, u32[]{:S(2)}, u32[]{:S(2)}) %all-to-all-start.1) | async-done | bytes 393248 | tf_op jit(solution)/shard_map/all_to_all | solution.py:280
  48.7 1.9 %collective-permute-start.3 = (bf16[8,4,24,128]{3,2,1,0:T(8,128)(2,1)S(1)}, bf16[8,4,24,128]{3,2,1,0:T(8,128)(2,1)S(1)}, u32[]{:S(2)}, u32[]{:S(2)}) collective-permute-start(bf16[8,4,24,128]{3,2,1,0:T(8,128)(2,1)S(1)} %get-tuple-element.43), channel_id=1, source_target_pairs={{0,1},{1,2},{2,3},{3,4},{4,5},{5,6},{6,7},{7,8},{8,9},{9,10},{10,1... | collective-permute-start | bytes 589832 | tf_op jit(solution)/shard_map/ppermute | solution.py:310
  50.7 5.5 %collective-permute-start.2 = (bf16[8,4,24,128]{3,2,1,0:T(8,128)(2,1)S(1)}, bf16[8,4,24,128]{3,2,1,0:T(8,128)(2,1)S(1)}, u32[]{:S(2)}, u32[]{:S(2)}) collective-permute-start(bf16[8,4,24,128]{3,2,1,0:T(8,128)(2,1)S(1)} %get-tuple-element.44), channel_id=1, source_target_pairs={{1,0},{2,1},{3,2},{4,3},{5,4},{6,5},{7,6},{8,7},{9,8},{10,9},{11,1... | collective-permute-start | bytes 589832 | tf_op jit(solution)/shard_map/ppermute | solution.py:311
  56.2 0.0 copy-done.8
  56.2 0.1 broadcast_in_dim.33.g_one_ref
  56.2 0.0 copy-done.9
  56.3 0.1 broadcast_in_dim.34.g_two_ref
  56.3 0.0 copy-start.2
  56.3 2.0 %own_rows.1 = (bf16[2,1152,256]{2,1,0:T(8,128)(2,1)S(1)}, bf16[2,576,256]{2,1,0:T(8,128)(2,1)S(1)}, f32[2,6,96,256]{3,2,1,0:T(8,128)S(1)}, f32[2,4,96,256]{3,2,1...) custom-call(bf16[16,4,24,128]{3,2,1,0:T(8,128)(2,1)S(1)} %all-to-all-done.1.own_ref, ...), custom_call_target="tpu_custom_call" | custom-call | flops 1000000000 | bytes 4000000 | tf_op jit(solution)/shard_map/own_rows/pallas_call | solution.py:136
  58.4 0.7 collective-permute-done.3.halo_ref
  59.1 0.0 copy-done.2
  59.1 1.7 %top_rows.1.rest_0_ = bf16[16,4,24,128]{3,2,1,0:T(8,128)(2,1)S(1)} custom-call(s32[2]{0:T(128)S(1)} %pad_add_fusion.place_ref, s32[64]{0:T(128)S(1)} %select_reduce_fusion.session_of_ref, s32[64]{0:T(128)S(1)} %copy-done.2, bf16[8,4,24,128]{3,2,1,0:T(8,128)(2,1)S(1)} %collective-permute-done.3.halo_ref, bf16[16,4,24,128]{3,2,1,0:T(8,128)(2,1)S(1)} %all-to-all-done.1.own_ref, ...), custom_call_target="tpu_custom_call" | custom-call | flops 1000000000 | bytes 4000000 | tf_op jit(solution)/shard_map/top_rows/pallas_call | solution.py:214
  60.7 0.1 collective-permute-done.2.halo_ref
  60.9 1.7 %bottom_rows.1 = bf16[16,4,24,128]{3,2,1,0:T(8,128)(2,1)S(1)} custom-call(s32[2]{0:T(128)S(1)} %pad_add_fusion.place_ref, s32[64]{0:T(128)S(1)} %select_reduce_fusion.session_of_ref, s32[64]{0:T(128)S(1)} %copy-done.2, bf16[8,4,24,128]{3,2,1,0:T(8,128)(2,1)S(1)} %collective-permute-done.2.halo_ref, ...), custom_call_target="tpu_custom_call", output_to_operand_aliasing={{}: (13, {})} | custom-call | flops 1000000000 | bytes 4000000 | tf_op jit(solution)/shard_map/bottom_rows/pallas_call | solution.py:214
  62.5 17.7 %all_to_all.20 = bf16[16,4,24,128]{3,2,1,0:T(8,128)(2,1)S(1)} all-to-all(bf16[16,4,24,128]{3,2,1,0:T(8,128)(2,1)S(1)} %bottom_rows.1), channel_id=1, replica_groups=mesh['sess'=16,'band'=32] {'sess'}, dimensions={0} | all-to-all | bytes 786432 | tf_op jit(solution)/shard_map/all_to_all | solution.py:280
  80.2 0.6 take_in_vmem.1
  80.8 17.2 %all_to_all.21 = bf16[16,4,24,128]{3,2,1,0:T(8,128)(2,1)S(1)} all-to-all(bf16[16,4,24,128]{3,2,1,0:T(8,128)(2,1)S(1)} %bitcast.29), channel_id=1, replica_groups=mesh['sess'=16,'band'=32] {'sess'}, dimensions={0} | all-to-all | bytes 786432 | tf_op jit(solution)/shard_map/all_to_all | solution.py:280
  98.0 1.1 %copy.22 = bf16[4,4,4,24,128]{4,0,3,1,2:T(4,128)(2,1)} copy(bf16[4,4,4,24,128]{4,3,2,1,0:T(8,128)(2,1)S(1)} %bitcast.30) | data formatting | bytes 786432 | tf_op jit(solution)/shard_map/reshape | solution.py:320
  (7 shorter events, 0.1 us)
Async XLA Ops:
  0.0 9.8 %copy-start.7 = (bf16[4,2,2,96,4,128]{5,4,3,2,1,0:T(4,128)(2,1)S(1)}, bf16[4,2,2,96,4,128]{5,4,3,2,1,0:T(4,128)(2,1)}, u32[]{:S(2)}) copy-start(bf16[4,2,2,96,4,128]{5,4,3,2,1,0:T(4,128)(2,1)} %param.10) | copy-start | bytes 4718596
  2.0 23.3 %all-to-all-start = ((bf16[16,4,24,128]{3,2,1,0:T(8,128)(2,1)}), bf16[16,4,24,128]{3,2,1,0:T(8,128)(2,1)S(1)}, u32[]{:S(2)}, u32[]{:S(2)}) async-start(bf16[16,4,24,128]{3,2,1,0:T(8,128)(2,1)} %bitcast.4), calls=%async_computation | async-start | bytes 786432 | tf_op jit(solution)/shard_map/all_to_all | solution.py:280
  10.2 14.9 %copy-start.3 = (s32[64]{0:T(128)S(1)}, s32[64]{0:T(128)}, u32[]{:S(2)}) copy-start(s32[64]{0:T(128)} %slots_ref.1) | copy-start | bytes 772
  11.1 23.0 %copy-start = (bf16[96,2592]{1,0:T(8,128)(2,1)S(1)}, bf16[96,2592]{1,0:T(8,128)(2,1)}, u32[]{:S(2)}) copy-start(bf16[96,2592]{1,0:T(8,128)(2,1)} %one_ref.1) | copy-start | bytes 1492996
  11.1 23.0 %copy-start.1 = (bf16[96,2592]{1,0:T(8,128)(2,1)S(1)}, bf16[96,2592]{1,0:T(8,128)(2,1)}, u32[]{:S(2)}) copy-start(bf16[96,2592]{1,0:T(8,128)(2,1)} %two_ref.1) | copy-start | bytes 1492996
  11.1 25.0 %collective-permute-start.1 = (bf16[3,4,2,96,128]{4,3,2,1,0:T(8,128)(2,1)}, bf16[3,4,2,96,128]{4,3,2,1,0:T(8,128)(2,1)}, u32[]{:S(2)}, u32[]{:S(2)}) collective-permute-start(bf16[3,4,2,96,128]{4,3,2,1,0:T(8,128)(2,1)} %pad_maximum_fusion.1), channel_id=1, source_target_pairs={{0,1},{1,2},{2,3},{3,4},{4,5},{5,6},{6,7},{7,8},{8,9},{9,10},{10,1... | collective-permute-start | bytes 1769480 | tf_op jit(solution)/shard_map/ppermute | solution.py:302
  16.2 22.0 %copy-start.6 = (s32[64]{0:T(128)S(1)}, s32[64]{0:T(128)}, u32[]{:S(2)}) copy-start(s32[64]{0:T(128)} %counts_ref.1) | copy-start | bytes 772
  16.2 21.9 %collective-permute-start = (bf16[3,4,2,96,128]{4,3,2,1,0:T(8,128)(2,1)}, bf16[3,4,2,96,128]{4,3,2,1,0:T(8,128)(2,1)}, u32[]{:S(2)}, u32[]{:S(2)}) collective-permute-start(bf16[3,4,2,96,128]{4,3,2,1,0:T(8,128)(2,1)} %pad_maximum_fusion), channel_id=1, source_target_pairs={{1,0},{2,1},{3,2},{4,3},{5,4},{6,5},{7,6},{8,7},{9,8},{10,9},{11,1... | collective-permute-start | bytes 1769480 | tf_op jit(solution)/shard_map/ppermute | solution.py:301
  26.7 22.0 %all-to-all-start.1 = ((bf16[16,4,24,128]{3,2,1,0:T(8,128)(2,1)}), bf16[16,4,24,128]{3,2,1,0:T(8,128)(2,1)S(1)}, u32[]{:S(2)}, u32[]{:S(2)}) async-start(bf16[16,4,24,128]{3,2,1,0:T(8,128)(2,1)} %bitcast.6), calls=%async_computation.1 | async-start | bytes 786432 | tf_op jit(solution)/shard_map/all_to_all | solution.py:280
  34.5 0.7 copy-start.4
  35.1 0.7 copy-start.5
  38.1 18.0 %copy-start.8 = (f32[96]{0:T(128)S(1)}, f32[96]{0:T(128)}, u32[]{:S(2)}) copy-start(f32[96]{0:T(128)} %param.16) | copy-start | bytes 1156
  38.1 18.1 %copy-start.9 = (f32[96]{0:T(128)S(1)}, f32[96]{0:T(128)}, u32[]{:S(2)}) copy-start(f32[96]{0:T(128)} %param.17) | copy-start | bytes 1156
  48.7 10.3 %collective-permute-start.3 = (bf16[8,4,24,128]{3,2,1,0:T(8,128)(2,1)S(1)}, bf16[8,4,24,128]{3,2,1,0:T(8,128)(2,1)S(1)}, u32[]{:S(2)}, u32[]{:S(2)}) collective-permute-start(bf16[8,4,24,128]{3,2,1,0:T(8,128)(2,1)S(1)} %get-tuple-element.43), channel_id=1, source_target_pairs={{0,1},{1,2},{2,3},{3,4},{4,5},{5,6},{6,7},{7,8},{8,9},{9,10},{10,1... | collective-permute-start | bytes 589832 | tf_op jit(solution)/shard_map/ppermute | solution.py:310
  50.7 10.2 %collective-permute-start.2 = (bf16[8,4,24,128]{3,2,1,0:T(8,128)(2,1)S(1)}, bf16[8,4,24,128]{3,2,1,0:T(8,128)(2,1)S(1)}, u32[]{:S(2)}, u32[]{:S(2)}) collective-permute-start(bf16[8,4,24,128]{3,2,1,0:T(8,128)(2,1)S(1)} %get-tuple-element.44), channel_id=1, source_target_pairs={{1,0},{2,1},{3,2},{4,3},{5,4},{6,5},{7,6},{8,7},{9,8},{10,9},{11,1... | collective-permute-start | bytes 589832 | tf_op jit(solution)/shard_map/ppermute | solution.py:311
  56.3 2.8 %copy-start.2 = (s32[64]{0:T(128)S(1)}, s32[64]{0:T(128)}, u32[]{:S(2)}) copy-start(s32[64]{0:T(128)} %active_ref.3) | copy-start | bytes 772
